TPU v7x, 256 devices: a whole 4x4x8 slice. The times are simulated.
256 devices in a mesh: gx: 8 (over y, x_lo), gy: 32 (over z, x_hi, core).
Axes of the slice: x: 4 (x_hi: 2, x_lo: 2; x = x_hi * 2 + x_lo), y: 4, z: 8, core: 2. Of those that a mesh axis runs over, the one named last changes fastest.
Arguments:
- features: bfloat16 [8, 32, 256, 256], P('gx', 'gy'), may hold values from -6 to 6
- displacement: float32 [8, 32, 3, 2048], P('gx', 'gy'), may hold values from -0.5 to 0.5, as said below
- neighbours: int32 [8, 32, 2048], P('gx', 'gy'), may hold values from 0 to 1791, as said below
- neighbour_count: int32 [8, 32, 256], P('gx', 'gy'), may hold values from 4 to 8, as said below
- species: int32 [8, 32, 256], P('gx', 'gy'), may hold values from 0 to 3
- send_list: int32 [8, 32, 8, 192], P('gx', 'gy'), may hold values from 0 to 255, as said below
- send_count: int32 [8, 32, 8], P('gx', 'gy'), may hold values from 96 to 192, as said below
- w_center: bfloat16 [256, 1024], replicated, may hold values from -0.375 to 0.375
- w_neighbour: bfloat16 [256, 1024], replicated, may hold values from -0.375 to 0.375
- w_radial: bfloat16 [8, 1024], replicated, may hold values from -4 to 4
- w_hidden: bfloat16 [1024, 1024], replicated, may hold values from -0.1875 to 0.1875
- w_tensor: bfloat16 [1024, 64], replicated, may hold values from -0.1875 to 0.1875
- readout: float32 [64], replicated, may hold values from -0.375 to 0.375
- species_scale: float32 [4], replicated, may hold values from 0.5 to 2
- species_shift: float32 [4], replicated, may hold values from -4 to 4
Outputs:
- atom_energy: float32 [8, 32, 256], P('gx', 'gy')
- forces: float32 [8, 32, 3, 256], P('gx', 'gy')
Inputs may be any that keep to these rules, and one draw needn't show every extreme that they name: `send_count`: For each direction some domain sends exactly 192 rows. `send_list`: each list holds distinct atoms in rising order. `neighbours`: rows 0..255 are own atoms, row 256 + b * 192 + k is row k of ghost block b; a ghost row always lies below the count of the list it came from. `neighbour_count`: some atom has all 8 slots live. `displacement`: each component's magnitude lies in 0.2 to 0.5.
All inputs are finite; a program needn't handle non-finite values.
Results may differ from a plain program's by a relative error of at most 0.018.
Values may be sent and summed in bfloat16 or wider, within the bound.
A program may use at most 128 MiB of HBM per device.

v0:
```python
import jax
import jax.numpy as jnp
from jax import lax
from jax.sharding import PartitionSpec as P

DIRECTIONS = ((-1, -1), (-1, 0), (-1, 1), (0, -1), (0, 1), (1, -1), (1, 0), (1, 1))


def passed_along(value, axis, steps):
    count = lax.axis_size(axis)
    pairs = [(source, (source + steps) % count) for source in range(count)]
    return lax.ppermute(value, axis, pairs)


def atom_energies(
    displace,
    centre_proj,
    table_proj,
    table_rows,
    neighbour_ids,
    live_mask,
    scale_atom,
    shift_atom,
    w_radial,
    w_hidden,
    w_tensor,
    readout,
):
    edge_total = displace.shape[1]
    atom_total = centre_proj.shape[0]
    per_atom = edge_total // atom_total
    channels = w_tensor.shape[1]
    basis_count = w_radial.shape[0]
    squared = jnp.sum(displace * displace, axis=0)
    distance = jnp.sqrt(squared)
    unit_vec = displace / distance[None, :]
    centres = (jnp.arange(basis_count).astype(jnp.float32) + 1.0) / basis_count
    basis_rows = jnp.exp(
        -jnp.square((distance[None, :] - centres[:, None]) * (0.5 * basis_count))
    ).astype(jnp.bfloat16)
    radial = lax.dot_general(
        basis_rows, w_radial, (((0,), (0,)), ((), ())), preferred_element_type=jnp.float32
    )
    centre_rows = jnp.broadcast_to(
        centre_proj[:, None, :], (atom_total, per_atom, centre_proj.shape[1])
    ).reshape(edge_total, centre_proj.shape[1])
    pre_act = (
        centre_rows.astype(jnp.float32)
        + jnp.take(table_proj, neighbour_ids, axis=0).astype(jnp.float32)
        + radial
    )
    first_layer = jax.nn.silu(pre_act).astype(jnp.bfloat16)
    second_layer = jax.nn.silu(
        jnp.dot(first_layer, w_hidden, preferred_element_type=jnp.float32)
    ).astype(jnp.bfloat16)
    tensor_wts = jnp.dot(second_layer, w_tensor, preferred_element_type=jnp.float32)
    gathered = jnp.take(table_rows, neighbour_ids, axis=0).astype(jnp.float32)
    scalar_part = gathered[:, :channels]
    vector_parts = [
        gathered[:, channels * (axis_num + 1) : channels * (axis_num + 2)] for axis_num in range(3)
    ]
    envelope = jnp.square(1.0 - squared) * live_mask
    weighted = tensor_wts * envelope[:, None]
    along_unit = (
        unit_vec[0][:, None] * vector_parts[0]
        + unit_vec[1][:, None] * vector_parts[1]
        + unit_vec[2][:, None] * vector_parts[2]
    )
    pieces = [weighted * (scalar_part + along_unit)]
    for axis_num in range(3):
        pieces.append(
            weighted * (scalar_part * unit_vec[axis_num][:, None] + vector_parts[axis_num])
        )
    invariant = jnp.zeros((atom_total, channels), jnp.float32)
    for member in pieces:
        invariant = invariant + jnp.square(
            member.reshape(atom_total, per_atom, channels).sum(axis=1)
        )
    return scale_atom * jnp.sum(invariant * readout[None, :], axis=1) + shift_atom


def domain_terms(
    own_rows,
    ghost_rows,
    displace,
    neighbour_ids,
    live_count,
    species_ids,
    w_center,
    w_neighbour,
    w_radial,
    w_hidden,
    w_tensor,
    readout,
    species_scale,
    species_shift,
):
    atom_total, row_width = own_rows.shape
    per_atom = displace.shape[1] // atom_total
    slot_count = ghost_rows.shape[1]
    table_rows = jnp.concatenate([own_rows, ghost_rows.reshape(8 * slot_count, row_width)], axis=0)
    centre_proj = jnp.dot(own_rows, w_center, preferred_element_type=jnp.float32).astype(
        jnp.bfloat16
    )
    table_proj = jnp.dot(table_rows, w_neighbour, preferred_element_type=jnp.float32).astype(
        jnp.bfloat16
    )
    live_mask = (
        (jnp.arange(per_atom)[None, :] < live_count[:, None]).astype(jnp.float32).reshape(-1)
    )
    species_hit = jnp.arange(species_scale.shape[0])[None, :] == species_ids[:, None]
    scale_atom = jnp.sum(jnp.where(species_hit, species_scale[None, :], 0.0), axis=1)
    shift_atom = jnp.sum(jnp.where(species_hit, species_shift[None, :], 0.0), axis=1)

    def energy_of(displaced):
        return atom_energies(
            displaced,
            centre_proj,
            table_proj,
            table_rows,
            neighbour_ids,
            live_mask,
            scale_atom,
            shift_atom,
            w_radial,
            w_hidden,
            w_tensor,
            readout,
        )

    energy, pullback = jax.vjp(energy_of, displace)
    edge_grad = pullback(jnp.ones_like(energy))[0]
    own_force = edge_grad.reshape(3, atom_total, per_atom).sum(axis=2)
    row_force = jax.ops.segment_sum(
        edge_grad.T, neighbour_ids, num_segments=atom_total + 8 * slot_count
    )
    own_force = own_force - row_force[:atom_total].T
    ghost_force = row_force[atom_total:].reshape(8, slot_count, 3).transpose(0, 2, 1)
    return (energy, own_force, ghost_force)


def shards(
    features,
    displacement,
    neighbours,
    neighbour_count,
    species,
    send_list,
    send_count,
    w_center,
    w_neighbour,
    w_radial,
    w_hidden,
    w_tensor,
    readout,
    species_scale,
    species_shift,
):
    own_rows = features[0, 0]
    atom_total = own_rows.shape[0]
    lists = send_list[0, 0]
    limits = send_count[0, 0]
    slot_count = lists.shape[1]
    picked = jnp.take(own_rows, lists.reshape(-1), axis=0).reshape(8, slot_count, own_rows.shape[1])
    keeping = jnp.arange(slot_count)[None, :] < limits[:, None]
    outgoing = jnp.where(keeping[:, :, None], picked, jnp.zeros_like(picked))
    ghosts = [None] * 8
    across = {}
    for stride in (1, -1):
        chosen = jnp.stack(
            [outgoing[DIRECTIONS.index((stride, offset_y))] for offset_y in (-1, 0, 1)]
        )
        across[stride] = passed_along(chosen, "gx", stride)
        ghosts[7 - DIRECTIONS.index((stride, 0))] = across[stride][1]
    for stride in (1, -1):
        facing = outgoing[DIRECTIONS.index((0, stride))]
        passing = jnp.stack([across[1][stride + 1], across[-1][stride + 1]])
        face_in = passed_along(facing, "gy", stride)
        corner_in = passed_along(passing, "gy", stride)
        ghosts[7 - DIRECTIONS.index((0, stride))] = face_in
        ghosts[7 - DIRECTIONS.index((1, stride))] = corner_in[0]
        ghosts[7 - DIRECTIONS.index((-1, stride))] = corner_in[1]
    energy, own_force, ghost_force = domain_terms(
        own_rows,
        jnp.stack(ghosts),
        displacement[0, 0],
        neighbours[0, 0],
        neighbour_count[0, 0],
        species[0, 0],
        w_center,
        w_neighbour,
        w_radial,
        w_hidden,
        w_tensor,
        readout,
        species_scale,
        species_shift,
    )
    returned = [None] * 8
    upward = {}
    for stride in (1, -1):
        chosen = jnp.stack(
            [ghost_force[DIRECTIONS.index((offset_x, stride))] for offset_x in (-1, 0, 1)]
        )
        upward[stride] = passed_along(chosen, "gy", stride)
        returned[DIRECTIONS.index((0, -stride))] = upward[stride][1]
    for stride in (1, -1):
        chosen = jnp.stack(
            [
                ghost_force[DIRECTIONS.index((stride, 0))],
                upward[1][stride + 1],
                upward[-1][stride + 1],
            ]
        )
        arrived = passed_along(chosen, "gx", stride)
        returned[DIRECTIONS.index((-stride, 0))] = arrived[0]
        returned[DIRECTIONS.index((-stride, -1))] = arrived[1]
        returned[DIRECTIONS.index((-stride, 1))] = arrived[2]
    back_rows = jnp.stack(returned).transpose(0, 2, 1).reshape(8 * slot_count, 3)
    forces = (
        own_force + jax.ops.segment_sum(back_rows, lists.reshape(-1), num_segments=atom_total).T
    )
    return (energy[None, None], forces[None, None])


def solution(mesh):
    placed = (
        P("gx", "gy", None, None),
        P("gx", "gy", None, None),
        P("gx", "gy", None),
        P("gx", "gy", None),
        P("gx", "gy", None),
        P("gx", "gy", None, None),
        P("gx", "gy", None),
        P(),
        P(),
        P(),
        P(),
        P(),
        P(),
        P(),
        P(),
    )
    return jax.shard_map(
        shards,
        mesh=mesh,
        in_specs=placed,
        out_specs=(P("gx", "gy", None), P("gx", "gy", None, None)),
        check_vma=False,
    )
```

profile of v0, /device:TPU:2, one launch (start us, length us, event | category | flops | bytes accessed | tf_op | source)
XLA Modules:
  0.0 173.7 jit_solution(10191813905837131509)
XLA Ops:
  0.7 0.9 reshape_squeeze.6
  3.1 4.6 %gather_fusion = bf16[1536,256]{1,0:T(8,128)(2,1)S(1)} fusion(bf16[256,256]{1,0:T(8,128)(2,1)} %bitcast.131, s32[2048]{0:T(1024)S(1)} %get-tuple-element.68), kind=kCustom, calls=%fused_computation | custom fusion | bytes 1579008 | tf_op jit(solution)/shard_map/jit(_take)/gather | solution.py:164
  8.4 0.9 fusion.77
  9.3 1.5 collective-permute-start
  10.9 0.8 collective-permute-start.1
  12.4 6.1 %collective-permute-start.5 = (bf16[192,256]{1,0:T(8,128)(2,1)}, bf16[192,256]{1,0:T(8,128)(2,1)S(1)}, u32[]{:S(2)}, u32[]{:S(2)}) collective-permute-start(bf16[192,256]{1,0:T(8,128)(2,1)} %get-tuple-element.28), channel_id=1, source_target_pairs={{0,31},{1,0},{2,1},{3,2},{4,3},{5,4},{6,5},{7,6},{8,7},{9,8},{10,9... | collective-permute-start | bytes 294920 | tf_op jit(solution)/shard_map/ppermute | solution.py:12
  19.5 4.6 %fusion.61 = f32[2048,1024]{1,0:T(8,128)} fusion(bf16[8,1024]{1,0:T(8,128)(2,1)S(1)} %copy-done.18, f32[8]{0:T(128)S(1)} %add_multiply_fusion, f32[2048]{0:T(1024)S(1)} %get-tuple-element.66), kind=kOutput, calls=%fused_computation.108 | convolution fusion | flops 33636352 | bytes 8413216 | tf_op jit(solution)/shard_map/jvp()/dot_general | solution.py:41
  25.4 2.3 %collective-permute-done.1 = bf16[3,192,256]{2,1,0:T(8,128)(2,1)S(1)} collective-permute-done((bf16[3,192,256]{2,1,0:T(8,128)(2,1)}, bf16[3,192,256]{2,1,0:T(8,128)(2,1)S(1)}, u32[]{:S(2)}, u32[]{:S(2)}) %collective-permute-start.1) | collective-permute-done | bytes 294944 | tf_op jit(solution)/shard_map/ppermute | solution.py:12
  27.7 0.9 slice.188
  28.8 1.4 fusion.42
  30.2 7.3 %collective-permute-done.2 = bf16[2,192,256]{2,1,0:T(8,128)(2,1)S(1)} collective-permute-done((bf16[2,192,256]{2,1,0:T(8,128)(2,1)S(1)}, bf16[2,192,256]{2,1,0:T(8,128)(2,1)S(1)}, u32[]{:S(2)}, u32[]{:S(2)}) %collective-permute-start.2) | collective-permute-done | bytes 196640 | tf_op jit(solution)/shard_map/ppermute | solution.py:12
  37.5 1.0 fusion.78
  38.8 3.1 %collective-permute-done.3 = bf16[2,192,256]{2,1,0:T(8,128)(2,1)S(1)} collective-permute-done((bf16[2,192,256]{2,1,0:T(8,128)(2,1)S(1)}, bf16[2,192,256]{2,1,0:T(8,128)(2,1)S(1)}, u32[]{:S(2)}, u32[]{:S(2)}) %collective-permute-start.3) | collective-permute-done | bytes 196640 | tf_op jit(solution)/shard_map/ppermute | solution.py:12
  41.9 0.9 bitcast_dynamic-update-slice_fusion.1
  42.9 0.9 copy-done.3
  43.8 9.0 %gather_fusion.2 = bf16[2048,256]{1,0:T(8,128)(2,1)} fusion(bf16[1792,256]{1,0:T(8,128)(2,1)S(1)} %pad_maximum_fusion, s32[2048]{0:T(1024)S(1)} %get-tuple-element.69), kind=kCustom, calls=%fused_computation.2 | custom fusion | bytes 2105344 | tf_op jit(solution)/shard_map/jvp(jit(_take))/gather | solution.py:57
  52.8 1.5 copy.61
  54.3 4.3 %convolution_convert_fusion = bf16[1792,1024]{1,0:T(8,128)(2,1)} fusion(bf16[256,1024]{1,0:T(8,128)(2,1)} %param.23, bf16[1536,256]{1,0:T(8,128)(2,1)} %bitcast.135, bf16[256,256]{1,0:T(8,128)(2,1)S(1)} %bitcast.133), kind=kOutput, calls=%fused_computation.31 | convolution fusion | flops 943194112 | bytes 5111808 | tf_op jit(solution)/shard_map/dot_general | solution.py:105
  58.6 13.5 %gather_fusion.1 = bf16[2048,1024]{1,0:T(8,128)(2,1)} fusion(bf16[1792,1024]{1,0:T(8,128)(2,1)} %convolution_convert_fusion, s32[2048]{0:T(1024)S(1)} %get-tuple-element.69), kind=kCustom, calls=%fused_computation.1 | custom fusion | bytes 8396800 | tf_op jit(solution)/shard_map/jvp(jit(_take))/gather | solution.py:49
  72.3 9.6 %fusion.17 = f32[2048,1024]{1,0:T(8,128)S(1)} fusion(bf16[1024,1024]{1,0:T(8,128)(2,1)S(1)} %copy-done, f32[2048,1024]{1,0:T(8,128)} %fusion.61, f32[256,1024]{1,0:T(8,128)} %fusion.42, bf16[2048,1024]{1,0:T(8,128)(2,1)} %gather_fusion.1, pred[2048]{0:T(1024)(128)(4,1)S(1)} %compare_and_fusion.1), kind=kOutput, calls=%fused_computation.29 | convolution fusion | flops 4313841664 | bytes 24119296 | tf_op jit(solution)/shard_map/jvp()/dot_general | solution.py:54
  82.0 4.1 %multiply_multiply_fusion.4 = (f32[2048,64]{0,1:T(8,128)}, f32[2048,64]{0,1:T(8,128)}, f32[2048,64]{0,1:T(8,128)}, f32[2048,64]{0,1:T(8,128)}, f32[2048,64]{0,1:T(8,128)}, /*index=5*/f32[2048,64]{0,1:T(8,128)}) fusion(f32[2048]{0:T(1024)S(1)} %get-tuple-element.65, f32[2048,256]{0,1:T(8,128)S(1)} %select_convert_fusion, f32[2048]{0:T(1024)S(1)} %bitcast.161, ...), kind=kOutput, calls=%fused_computation.73 | convolution fusion | flops 281149440 | bytes 13795328 | tf_op jit(solution)/shard_map/jvp()/dot_general | solution.py:56
  86.2 1.4 copy.62
  87.9 1.4 copy.65
  89.2 1.0 bitcast_reduce_fusion
  90.2 1.4 copy.64
  91.6 1.0 bitcast_reduce_fusion.1
  92.6 1.4 copy.63
  94.3 1.8 %multiply_multiply_fusion.5 = (f32[256,64]{1,0:T(8,128)S(1)}, f32[256]{0:T(256)S(1)}, f32[256,64]{1,0:T(8,128)}, f32[256,64]{1,0:T(8,128)}, f32[256,64]{1,0:T(8,128)S(1)}) fusion(f32[256,64]{1,0:T(8,128)S(1)} %bitcast_reduce_fusion.3, f32[256]{0:T(256)S(1)} %copy-done.20, f32[64]{0:T(128)S(1)} %copy-done.28, f32[256,64]{1,0:T(8,128)} %bitcast_reduce_fusion, ...), kind=kLoop, calls=%fused_computation.74 | loop fusion | flops 294656 | bytes 526592 | tf_op jit(solution)/shard_map/transpose(jvp())/mul | solution.py:76
  96.2 1.1 copy.66
  97.3 1.0 broadcast_bitcast_fusion.2
  98.3 1.1 copy.67
  99.4 1.0 broadcast_bitcast_fusion.1
  100.4 1.1 copy.68
  101.6 1.1 copy.69
  102.7 3.9 %multiply_reduce_fusion.6 = (f32[2048]{0:T(1024)S(1)}, f32[2048]{0:T(1024)S(1)}, f32[2048]{0:T(1024)S(1)}, f32[2048]{0:T(1024)S(1)}, f32[2048]{0:T(1024)S(1)}, /...) fusion(f32[2048,64]{0,1:T(8,128)} %copy.66, f32[2048,256]{0,1:T(8,128)} %copy-done.2, ...), kind=kLoop, calls=%fused_computation.61 | loop fusion | flops 4179968 | bytes 5857280 | tf_op jit(solution)/shard_map/transpose(jvp())/reduce_sum | solution.py:72
  106.6 10.9 %fusion.1 = bf16[2048,1024]{1,0:T(8,128)(2,1)} fusion(bf16[1024,1024]{1,0:T(8,128)(2,1)S(1)} %copy-done, f32[2048,1024]{1,0:T(8,128)} %copy-done.33, bf16[1024,64]{0,1:T(8,128)(2,1)S(1)} %copy-done.32, f32[2048,64]{0,1:T(8,128)} %get-tuple-element.22, f32[2048]{0:T(1024)S(1)} %get-tuple-element.65), kind=kOutput, calls=%fused_computation.12 | convolution fusion | flops 4586602496 | bytes 15343616 | tf_op jit(solution)/shard_map/transpose(jvp())/dot_general | solution.py:54
  117.5 8.4 %fusion.43 = f32[2048]{0:T(1024)S(1)} fusion(bf16[8,1024]{1,0:T(8,128)(2,1)S(1)} %copy-done.19, f32[2048,1024]{1,0:T(8,128)} %fusion.61, bf16[2048,1024]{1,0:T(8,128)(2,1)} %fusion.1, f32[256,1024]{1,0:T(8,128)S(1)} %copy-done.4, bf16[2048,1024]{1,0:T(8,128)(2,1)} %gather_fusion.1, pred[2048]{0:T(1024)(128)(4,1)S(1)} %copy-done.22, f32[8]{0:T(128)S(1)} %copy-done.25, ...), kind=kOutput, calls=%fused_computation.42 | convolution fusion | flops 65189888 | bytes 17860640 | tf_op jit(solution)/shard_map/transpose(jvp())/dot_general | solution.py:41
  126.2 1.4 copy.74
  127.6 12.0 %scatter_custom_fusion = f32[1792,3]{1,0:T(8,128)S(1)} fusion(s32[2048]{0:T(1024)} %bitcast.165, f32[2048,3]{1,0:T(8,128)} %copy.74, f32[]{:T(128)} %constant.30.clone.1), kind=kCustom, calls=%fused_computation.67 | custom fusion | flops 6144 | bytes 22016 | tf_op jit(solution)/shard_map/scatter-add | solution.py:134
  139.6 0.9 slice.209
  140.6 1.5 copy.76
  142.1 5.6 %collective-permute-start.7 = (f32[3,3,192]{2,1,0:T(4,128)S(1)}, f32[3,3,192]{2,1,0:T(4,128)S(1)}, u32[]{:S(2)}, u32[]{:S(2)}) collective-permute-start(f32[3,3,192]{2,1,0:T(4,128)S(1)} %pad_maximum_fusion.4), channel_id=1, source_target_pairs={{0,31},{1,0},{2,1},{3,2},{4,3},{5,4},{6,5},{7,6},{8,7},{9,8},{10,9... | collective-permute-start | bytes 20744 | tf_op jit(solution)/shard_map/ppermute | solution.py:12
  149.1 6.5 %collective-permute-done.6 = f32[3,3,192]{2,1,0:T(4,128)S(1)} collective-permute-done((f32[3,3,192]{2,1,0:T(4,128)S(1)}, f32[3,3,192]{2,1,0:T(4,128)S(1)}, u32[]{:S(2)}, u32[]{:S(2)}) %collective-permute-start.6) | collective-permute-done | bytes 6944 | tf_op jit(solution)/shard_map/ppermute | solution.py:12
  155.6 2.2 %collective-permute-start.8 = (f32[3,3,192]{2,1,0:T(4,128)S(1)}, f32[3,3,192]{2,1,0:T(4,128)S(1)}, u32[]{:S(2)}, u32[]{:S(2)}) collective-permute-start(f32[3,3,192]{2,1,0:T(4,128)S(1)} %pad_maximum_fusion.5), channel_id=1, source_target_pairs={{0,32},{32,64},{64,96},{96,128},{128,160},{160,192},{192,224},{224... | collective-permute-start | bytes 20744 | tf_op jit(solution)/shard_map/ppermute | solution.py:12
  158.0 1.4 collective-permute-done.8
  159.4 3.1 %collective-permute-done.9 = f32[3,3,192]{2,1,0:T(4,128)S(1)} collective-permute-done((f32[3,3,192]{2,1,0:T(4,128)S(1)}, f32[3,3,192]{2,1,0:T(4,128)S(1)}, u32[]{:S(2)}, u32[]{:S(2)}) %collective-permute-start.9) | collective-permute-done | bytes 6944 | tf_op jit(solution)/shard_map/ppermute | solution.py:12
  162.6 1.2 copy.85
  163.8 9.1 %scatter_custom_fusion.1 = f32[256,3]{1,0:T(8,128)S(1)} fusion(s32[1536]{0:T(1024)} %reshape.283, f32[1536,3]{1,0:T(8,128)} %bitcast.138, f32[]{:T(128)} %constant.30.clone.1), kind=kCustom, calls=%fused_computation.103 | custom fusion | flops 4608 | bytes 3584 | tf_op jit(solution)/shard_map/scatter-add | solution.py:221
  (135 shorter events, 9.2 us)
Async XLA Ops:
  0.6 71.6 %copy-start = (bf16[1024,1024]{1,0:T(8,128)(2,1)S(1)}, bf16[1024,1024]{1,0:T(8,128)(2,1)}, u32[]{:S(2)}) copy-start(bf16[1024,1024]{1,0:T(8,128)(2,1)} %param.25) | copy-start | bytes 6291460
  0.6 17.8 %copy-start.5 = (f32[1,1,3,2048]{3,1,2,0:T(1,128)S(1)}, f32[1,1,3,2048]{3,1,2,0:T(1,128)}, u32[]{:S(2)}) copy-start(f32[1,1,3,2048]{3,1,2,0:T(1,128)} %param.16) | copy-start | bytes 73732
  0.7 17.8 %copy-start.26 = (s32[1,1,256]{2,1,0:T(1,128)S(1)}, s32[1,1,256]{2,1,0:T(1,128)}, u32[]{:S(2)}) copy-start(s32[1,1,256]{2,1,0:T(1,128)} %param.18) | copy-start | bytes 3076
  0.7 18.7 %copy-start.18 = (bf16[8,1024]{1,0:T(8,128)(2,1)S(1)}, bf16[8,1024]{1,0:T(8,128)(2,1)}, u32[]{:S(2)}) copy-start(bf16[8,1024]{1,0:T(8,128)(2,1)} %param.24) | copy-start | bytes 49156
  8.3 15.7 %copy-start.7 = (s32[1,1,8,192]{3,2,1,0:T(8,128)S(1)}, s32[1,1,8,192]{3,2,1,0:T(8,128)}, u32[]{:S(2)}) copy-start(s32[1,1,8,192]{3,2,1,0:T(8,128)} %param.20) | copy-start | bytes 18436
  8.4 16.4 %copy-start.27 = (s32[1,1,256]{2,1,0:T(1,128)S(1)}, s32[1,1,256]{2,1,0:T(1,128)}, u32[]{:S(2)}) copy-start(s32[1,1,256]{2,1,0:T(1,128)} %param.19) | copy-start | bytes 3076
  8.4 16.4 %copy-start.29 = (f32[4]{0:T(128)S(1)}, f32[4]{0:T(128)}, u32[]{:S(2)}) copy-start(f32[4]{0:T(128)} %param.28) | copy-start | bytes 52
  8.4 16.4 %copy-start.30 = (f32[4]{0:T(128)S(1)}, f32[4]{0:T(128)}, u32[]{:S(2)}) copy-start(f32[4]{0:T(128)} %param.29) | copy-start | bytes 52
  9.3 19.4 %copy-start.1 = (bf16[1,1,256,256]{3,2,1,0:T(8,128)(2,1)S(1)}, bf16[1,1,256,256]{3,2,1,0:T(8,128)(2,1)}, u32[]{:S(2)}) copy-start(bf16[1,1,256,256]{3,2,1,0:T(8,128)(2,1)} %param.15) | copy-start | bytes 393220
  9.3 19.5 %copy-start.6 = (bf16[256,1024]{1,0:T(8,128)(2,1)S(1)}, bf16[256,1024]{1,0:T(8,128)(2,1)}, u32[]{:S(2)}) copy-start(bf16[256,1024]{1,0:T(8,128)(2,1)} %param.22) | copy-start | bytes 1572868
  9.3 18.4 %collective-permute-start = (bf16[3,192,256]{2,1,0:T(8,128)(2,1)}, bf16[3,192,256]{2,1,0:T(8,128)(2,1)}, u32[]{:S(2)}, u32[]{:S(2)}) collective-permute-start(bf16[3,192,256]{2,1,0:T(8,128)(2,1)} %get-tuple-element.30), channel_id=1, source_target_pairs={{0,32},{32,64},{64,96},{96,128},{128,160},{160,192},{192,224},{224... | collective-permute-start | bytes 884744 | tf_op jit(solution)/shard_map/ppermute | solution.py:12
  10.9 16.9 %collective-permute-start.1 = (bf16[3,192,256]{2,1,0:T(8,128)(2,1)}, bf16[3,192,256]{2,1,0:T(8,128)(2,1)S(1)}, u32[]{:S(2)}, u32[]{:S(2)}) collective-permute-start(bf16[3,192,256]{2,1,0:T(8,128)(2,1)} %get-tuple-element.31), channel_id=1, source_target_pairs={{0,224},{32,0},{64,32},{96,64},{128,96},{160,128},{192,160},{224,1... | collective-permute-start | bytes 884744 | tf_op jit(solution)/shard_map/ppermute | solution.py:12
  12.4 29.5 %collective-permute-start.4 = (bf16[192,256]{1,0:T(8,128)(2,1)}, bf16[192,256]{1,0:T(8,128)(2,1)}, u32[]{:S(2)}, u32[]{:S(2)}) collective-permute-start(bf16[192,256]{1,0:T(8,128)(2,1)} %get-tuple-element.29), channel_id=1, source_target_pairs={{0,1},{1,2},{2,3},{3,4},{4,5},{5,6},{6,7},{7,8},{8,9},{9,10},{10,1... | collective-permute-start | bytes 294920 | tf_op jit(solution)/shard_map/ppermute | solution.py:12
  12.4 30.5 %collective-permute-start.5 = (bf16[192,256]{1,0:T(8,128)(2,1)}, bf16[192,256]{1,0:T(8,128)(2,1)S(1)}, u32[]{:S(2)}, u32[]{:S(2)}) collective-permute-start(bf16[192,256]{1,0:T(8,128)(2,1)} %get-tuple-element.28), channel_id=1, source_target_pairs={{0,31},{1,0},{2,1},{3,2},{4,3},{5,4},{6,5},{7,6},{8,7},{9,8},{10,9... | collective-permute-start | bytes 294920 | tf_op jit(solution)/shard_map/ppermute | solution.py:12
  18.5 6.9 %copy-start.24 = (f32[8]{0:T(128)}, f32[8]{0:T(128)S(1)}, u32[]{:S(2)}) copy-start(f32[8]{0:T(128)S(1)} %add_multiply_fusion) | copy-start | bytes 100
  18.7 0.6 copy-start.16
  19.4 62.5 %copy-start.8 = (f32[1,2048]{1,0:T(1,128)}, f32[1,2048]{1,0:T(1,128)S(1)}, u32[]{:S(2)}) copy-start(f32[1,2048]{1,0:T(1,128)S(1)} %get-tuple-element.49) | copy-start | bytes 24580
  19.4 62.5 %copy-start.10 = (f32[1,2048]{1,0:T(1,128)}, f32[1,2048]{1,0:T(1,128)S(1)}, u32[]{:S(2)}) copy-start(f32[1,2048]{1,0:T(1,128)S(1)} %get-tuple-element.50) | copy-start | bytes 24580
  19.4 62.5 %copy-start.12 = (f32[1,2048]{1,0:T(1,128)}, f32[1,2048]{1,0:T(1,128)S(1)}, u32[]{:S(2)}) copy-start(f32[1,2048]{1,0:T(1,128)S(1)} %get-tuple-element.51) | copy-start | bytes 24580
  19.4 19.3 %copy-start.14 = (s32[1,1,2048]{2,1,0:T(1,128)S(1)}, s32[1,1,2048]{2,1,0:T(1,128)}, u32[]{:S(2)}) copy-start(s32[1,1,2048]{2,1,0:T(1,128)} %param.17) | copy-start | bytes 24580
  28.7 8.8 %collective-permute-start.2 = (bf16[2,192,256]{2,1,0:T(8,128)(2,1)S(1)}, bf16[2,192,256]{2,1,0:T(8,128)(2,1)S(1)}, u32[]{:S(2)}, u32[]{:S(2)}) collective-permute-start(bf16[2,192,256]{2,1,0:T(8,128)(2,1)S(1)} %pad_maximum_fusion.1), channel_id=1, source_target_pairs={{0,1},{1,2},{2,3},{3,4},{4,5},{5,6},{6,7},{7,8},{8,9},{9,10},{10,1... | collective-permute-start | bytes 589832 | tf_op jit(solution)/shard_map/ppermute | solution.py:12
  38.4 3.5 %collective-permute-start.3 = (bf16[2,192,256]{2,1,0:T(8,128)(2,1)S(1)}, bf16[2,192,256]{2,1,0:T(8,128)(2,1)S(1)}, u32[]{:S(2)}, u32[]{:S(2)}) collective-permute-start(bf16[2,192,256]{2,1,0:T(8,128)(2,1)S(1)} %pad_maximum_fusion.2), channel_id=1, source_target_pairs={{0,31},{1,0},{2,1},{3,2},{4,3},{5,4},{6,5},{7,6},{8,7},{9,8},{10,9... | collective-permute-start | bytes 589832 | tf_op jit(solution)/shard_map/ppermute | solution.py:12
  38.7 33.5 %copy-start.21 = (pred[2048]{0:T(1024)(128)(4,1)}, pred[2048]{0:T(1024)(128)(4,1)S(1)}, u32[]{:S(2)}) copy-start(pred[2048]{0:T(1024)(128)(4,1)S(1)} %compare_and_fusion.1) | copy-start | bytes 6148
  42.9 0.9 copy-start.3
  72.3 9.7 %copy-start.2 = (f32[2048,256]{0,1:T(8,128)}, f32[2048,256]{0,1:T(8,128)S(1)}, u32[]{:S(2)}) copy-start(f32[2048,256]{0,1:T(8,128)S(1)} %select_convert_fusion) | copy-start | bytes 6291460
  72.3 9.7 %copy-start.31 = (bf16[1024,64]{0,1:T(8,128)(2,1)S(1)}, bf16[1024,64]{0,1:T(8,128)(2,1)}, u32[]{:S(2)}) copy-start(bf16[1024,64]{0,1:T(8,128)(2,1)} %param.26) | copy-start | bytes 393220
  82.0 4.2 %copy-start.33 = (f32[2048,1024]{1,0:T(8,128)}, f32[2048,1024]{1,0:T(8,128)S(1)}, u32[]{:S(2)}) copy-start(f32[2048,1024]{1,0:T(8,128)S(1)} %fusion.17) | copy-start | bytes 25165828
  86.1 8.1 %copy-start.20 = (f32[256]{0:T(256)S(1)}, f32[256]{0:T(256)}, u32[]{:S(2)}) copy-start(f32[256]{0:T(256)} %get-tuple-element.20) | copy-start | bytes 3076
  86.1 8.1 %copy-start.28 = (f32[64]{0:T(128)S(1)}, f32[64]{0:T(128)}, u32[]{:S(2)}) copy-start(f32[64]{0:T(128)} %param.27) | copy-start | bytes 772
  91.6 11.1 %copy-start.9 = (f32[1,2048]{1,0:T(1,128)S(1)}, f32[1,2048]{1,0:T(1,128)}, u32[]{:S(2)}) copy-start(f32[1,2048]{1,0:T(1,128)} %copy-done.8) | copy-start | bytes 24580
  91.6 11.1 %copy-start.11 = (f32[1,2048]{1,0:T(1,128)S(1)}, f32[1,2048]{1,0:T(1,128)}, u32[]{:S(2)}) copy-start(f32[1,2048]{1,0:T(1,128)} %copy-done.10) | copy-start | bytes 24580
  91.6 11.1 %copy-start.13 = (f32[1,2048]{1,0:T(1,128)S(1)}, f32[1,2048]{1,0:T(1,128)}, u32[]{:S(2)}) copy-start(f32[1,2048]{1,0:T(1,128)} %copy-done.12) | copy-start | bytes 24580
  96.1 10.5 %copy-start.32 = (bf16[1024,64]{0,1:T(8,128)(2,1)S(1)}, bf16[1024,64]{0,1:T(8,128)(2,1)}, u32[]{:S(2)}) copy-start(bf16[1024,64]{0,1:T(8,128)(2,1)} %param.26) | copy-start | bytes 393220
  106.6 10.9 %copy-start.4 = (f32[256,1024]{1,0:T(8,128)S(1)}, f32[256,1024]{1,0:T(8,128)}, u32[]{:S(2)}) copy-start(f32[256,1024]{1,0:T(8,128)} %fusion.42) | copy-start | bytes 3145732
  106.6 10.9 %copy-start.19 = (bf16[8,1024]{1,0:T(8,128)(2,1)S(1)}, bf16[8,1024]{1,0:T(8,128)(2,1)}, u32[]{:S(2)}) copy-start(bf16[8,1024]{1,0:T(8,128)(2,1)} %param.24) | copy-start | bytes 49156
  106.6 10.9 %copy-start.22 = (pred[2048]{0:T(1024)(128)(4,1)S(1)}, pred[2048]{0:T(1024)(128)(4,1)}, u32[]{:S(2)}) copy-start(pred[2048]{0:T(1024)(128)(4,1)} %copy-done.21) | copy-start | bytes 6148
  106.6 10.9 %copy-start.25 = (f32[8]{0:T(128)S(1)}, f32[8]{0:T(128)}, u32[]{:S(2)}) copy-start(f32[8]{0:T(128)} %copy-done.24) | copy-start | bytes 100
  117.5 8.5 %copy-start.15 = (f32[2048]{0:T(1024)S(1)}, f32[2048]{0:T(1024)}, u32[]{:S(2)}) copy-start(f32[2048]{0:T(1024)} %get-tuple-element.64) | copy-start | bytes 24580
  117.5 8.5 %copy-start.17 = (pred[2048]{0:T(1024)(128)(4,1)S(1)}, pred[2048]{0:T(1024)(128)(4,1)}, u32[]{:S(2)}) copy-start(pred[2048]{0:T(1024)(128)(4,1)} %copy-done.16) | copy-start | bytes 6148
  117.5 30.1 %copy-start.23 = (f32[256]{0:T(256)S(1)}, f32[256]{0:T(256)}, u32[]{:S(2)}) copy-start(f32[256]{0:T(256)} %get-tuple-element.21) | copy-start | bytes 3076
  142.1 7.0 %collective-permute-start.7 = (f32[3,3,192]{2,1,0:T(4,128)S(1)}, f32[3,3,192]{2,1,0:T(4,128)S(1)}, u32[]{:S(2)}, u32[]{:S(2)}) collective-permute-start(f32[3,3,192]{2,1,0:T(4,128)S(1)} %pad_maximum_fusion.4), channel_id=1, source_target_pairs={{0,31},{1,0},{2,1},{3,2},{4,3},{5,4},{6,5},{7,6},{8,7},{9,8},{10,9... | collective-permute-start | bytes 20744 | tf_op jit(solution)/shard_map/ppermute | solution.py:12
  148.8 6.8 %collective-permute-start.6 = (f32[3,3,192]{2,1,0:T(4,128)S(1)}, f32[3,3,192]{2,1,0:T(4,128)S(1)}, u32[]{:S(2)}, u32[]{:S(2)}) collective-permute-start(f32[3,3,192]{2,1,0:T(4,128)S(1)} %pad_maximum_fusion.3), channel_id=1, source_target_pairs={{0,1},{1,2},{2,3},{3,4},{4,5},{5,6},{6,7},{7,8},{8,9},{9,10},{10,1... | collective-permute-start | bytes 20744 | tf_op jit(solution)/shard_map/ppermute | solution.py:12
  155.6 3.8 %collective-permute-start.8 = (f32[3,3,192]{2,1,0:T(4,128)S(1)}, f32[3,3,192]{2,1,0:T(4,128)S(1)}, u32[]{:S(2)}, u32[]{:S(2)}) collective-permute-start(f32[3,3,192]{2,1,0:T(4,128)S(1)} %pad_maximum_fusion.5), channel_id=1, source_target_pairs={{0,32},{32,64},{64,96},{96,128},{128,160},{160,192},{192,224},{224... | collective-permute-start | bytes 20744 | tf_op jit(solution)/shard_map/ppermute | solution.py:12
  157.9 4.7 %collective-permute-start.9 = (f32[3,3,192]{2,1,0:T(4,128)S(1)}, f32[3,3,192]{2,1,0:T(4,128)S(1)}, u32[]{:S(2)}, u32[]{:S(2)}) collective-permute-start(f32[3,3,192]{2,1,0:T(4,128)S(1)} %pad_maximum_fusion.6), channel_id=1, source_target_pairs={{0,224},{32,0},{64,32},{96,64},{128,96},{160,128},{192,160},{224,1... | collective-permute-start | bytes 20744 | tf_op jit(solution)/shard_map/ppermute | solution.py:12
where the time goes:
time: 174 us
  local copies, waits for them, and re-layouts  53.9 us (31%)
  matrix products  43.3 us (25%)
  other arithmetic  34.3 us (20%)
  waiting for transfers between devices  24 us (14%)
  starting transfers between devices  16.7 us (10%)
    ppermute x10, waiting for transfers between devices, passed_along(): return lax.ppermute(value, axis, pairs)  24 us
    dot_general x2, matrix products, atom_energies(): jnp.dot(first_layer, w_hidden, preferred_element_type=jnp.float32)  20.5 us
    ppermute x10, starting transfers between devices, passed_along(): return lax.ppermute(value, axis, pairs)  16.7 us
    gather x1, local copies, waits for them, and re-layouts, atom_energies(): jnp.take(table_proj, neighbour_ids, axis=0).astype(jnp.float32)  13.5 us
    dot_general x2, matrix products, atom_energies(): lax.dot_general(basis_rows, w_radial, (((0,), (0,)), ((), ())), preferred...  13 us
    scatter-add x1, other arithmetic, domain_terms(): jax.ops.segment_sum(edge_grad.T, neighbour_ids, num_segments=atom_total +...  12 us
    gather x2, local copies, waits for them, and re-layouts, atom_energies(): gathered = jnp.take(table_rows, neighbour_ids, axis=0).astype(jnp.float32)  10.5 us
    scatter-add x1, other arithmetic, shards(): jax.ops.segment_sum(back_rows, lists.reshape(-1), num_segments=atom_total)  9.15 us
  transfers between devices with their start and end apart: 10, of which 7 were waited for; matrix products, arithmetic and copies ran while one was open for 7% of the time, Pallas kernels for 0%

commit v1 on v0

v1 whole, which is shorter than its diff:
```python
import jax
import jax.numpy as jnp
from jax import lax
from jax.experimental import pallas as pl
from jax.experimental.pallas import tpu as pltpu
from jax.sharding import PartitionSpec as P

DIRECTIONS = ((-1, -1), (-1, 0), (-1, 1), (0, -1), (0, 1), (1, -1), (1, 0), (1, 1))
ATOMS = 256
SLOTS = 8
EDGES = ATOMS * SLOTS
GHOSTS = 192
WIDTH = 256
HID = 1024
CH = 64
F32 = jnp.float32
BF16 = jnp.bfloat16
MESH = pl.DeviceIdType.MESH


def iota(shape, dim):
    return lax.broadcasted_iota(jnp.int32, shape, dim)


def one_hot(hit):
    return jnp.where(hit, 1.0, 0.0).astype(BF16)


def dot(a, b):
    return jnp.dot(a, b, preferred_element_type=F32)


def silu_pair(value):
    gate = 0.5 * jnp.tanh(0.5 * value) + 0.5
    act = value * gate
    return act, gate + act * (1.0 - gate)


def split(value):
    high = value.astype(BF16)
    return high, (value - high.astype(F32)).astype(BF16)


def kernel(
    feat,
    disp,
    nbr,
    cnt,
    spc,
    lists,
    scnt,
    wc_hbm,
    wn_hbm,
    wr,
    wh_hbm,
    wt_hbm,
    ro,
    sscale,
    sshift,
    en_ref,
    fo_ref,
    wc,
    wn,
    wh,
    wt,
    wct,
    wnt,
    wrt,
    wht,
    wtt,
    sel,
    outg,
    ghost,
    tg,
    stage,
    dsp,
    geo,
    oh,
    pre,
    drad,
    rows,
    act1,
    act2,
    tws,
    grads,
    back_out,
    back_in,
    load_sem,
    send_sem,
    recv_sem,
    bsend_sem,
    brecv_sem,
):
    px, qy = lax.axis_index("gx"), lax.axis_index("gy")
    nx, ny = lax.axis_size("gx"), lax.axis_size("gy")
    peers = [
        (lax.rem(px + (ox + nx), nx), lax.rem(qy + (oy + ny), ny)) for ox, oy in DIRECTIONS
    ]
    loads = [
        pltpu.make_async_copy(src, dst, load_sem.at[num])
        for num, (src, dst) in enumerate(
            ((wc_hbm, wc), (wn_hbm, wn), (wh_hbm, wh), (wt_hbm, wt))
        )
    ]
    for load in loads:
        load.start()
    barrier = pltpu.get_barrier_semaphore()
    for peer in peers:
        pl.semaphore_signal(barrier, inc=1, device_id=peer, device_id_type=MESH)

    kept = jnp.where(
        iota((GHOSTS, 8), 0) < scnt[...], jnp.transpose(lists[...].astype(F32)), -1.0
    )
    lane = iota((GHOSTS, ATOMS), 1).astype(F32)
    for num in range(8):
        hit = one_hot(kept[:, num : num + 1] == lane)
        sel[num] = hit
        outg[num] = dot(hit, feat[...]).astype(BF16)
    pl.semaphore_wait(barrier, 8)
    sends = []
    for num in range(8):
        copy = pltpu.make_async_remote_copy(
            src_ref=outg.at[num],
            dst_ref=ghost.at[7 - num],
            send_sem=send_sem.at[num],
            recv_sem=recv_sem.at[7 - num],
            device_id=peers[num],
            device_id_type=MESH,
        )
        copy.start()
        sends.append(copy)

    for axis in range(3):
        for c in range(16):
            stage[pl.ds(axis * 16 + c, 1), :] = disp[axis : axis + 1, c * 128 : (c + 1) * 128]
    for c in range(16):
        stage[pl.ds(48 + c, 1), :] = nbr[0:1, c * 128 : (c + 1) * 128].astype(F32)
    turned = jnp.transpose(stage[...])
    for row in range(4):
        for a in range(16):
            dsp[row, :, a * 16 : (a + 1) * 16] = turned[
                a * 8 : (a + 1) * 8, row * 16 : (row + 1) * 16
            ]
    col = iota((ATOMS, ATOMS), 1)
    swap = iota((ATOMS, ATOMS), 0) == (col & 15) * 16 + (col >> 4)
    swap_b = one_hot(swap)
    small = jnp.concatenate(
        [cnt[...].astype(F32), spc[...].astype(F32), jnp.zeros((14, ATOMS), F32)], axis=0
    ).astype(BF16)
    small = dot(small, swap_b)
    count, kind = small[0:1], small[1:2]
    scale = jnp.zeros((1, ATOMS), F32)
    shift = jnp.zeros((1, ATOMS), F32)
    for num in range(4):
        hit = kind == float(num)
        scale = jnp.where(hit, sscale[0:1, num : num + 1], scale)
        shift = jnp.where(hit, sshift[0:1, num : num + 1], shift)
    squared = dsp[0] * dsp[0] + dsp[1] * dsp[1] + dsp[2] * dsp[2]
    distance = jnp.sqrt(squared)
    inverse = 1.0 / distance
    live = jnp.where(iota((SLOTS, ATOMS), 0).astype(F32) < count, 1.0, 0.0)
    for axis in range(3):
        geo[axis] = dsp[axis] * inverse
    geo[3] = jnp.square(1.0 - squared) * live
    geo[4] = distance
    geo[5] = -4.0 * (1.0 - squared) * live
    geo[6] = inverse

    wrt[...] = jnp.transpose(
        jnp.concatenate([wr[...].astype(F32), jnp.zeros((120, HID), F32)], axis=0)
    ).astype(BF16)
    loads[0].wait()
    for num in range(4):
        wct[num * 256 : (num + 1) * 256, :] = jnp.transpose(wc[:, num * 256 : (num + 1) * 256])
    loads[1].wait()
    for num in range(4):
        wnt[num * 256 : (num + 1) * 256, :] = jnp.transpose(wn[:, num * 256 : (num + 1) * 256])
    loads[2].wait()

    def turn(num, carry):
        start = pl.multiple_of(num * 256, 256)
        for part in range(4):
            wht[pl.ds(start, 256), part * 256 : (part + 1) * 256] = jnp.transpose(
                wh[part * 256 : (part + 1) * 256, pl.ds(start, 256)]
            )
        return carry

    lax.fori_loop(0, 4, turn, 0)
    loads[3].wait()
    for part in range(4):
        wtt[:, part * 256 : (part + 1) * 256] = jnp.transpose(wt[part * 256 : (part + 1) * 256, :])

    feat_t = jnp.transpose(feat[...])
    feat_p = dot(feat_t, swap_b).astype(BF16)
    unit_id = iota((16, ATOMS), 0)
    centre_at = (unit_id.astype(F32) + 1.0) * 0.125
    row_id = iota((256, ATOMS), 0).astype(F32)

    def before(k, carry):
        lanes = pl.ds(pl.multiple_of(k * 256, 256), 256)
        ids = dsp[3, pl.ds(k, 1), :]
        for part in range(7):
            oh[part * 256 : (part + 1) * 256, lanes] = one_hot(row_id + (part * 256.0) == ids)
        rows[:, lanes] = dot(feat_t, oh[0:256, lanes]).astype(BF16)
        offset = (geo[4, pl.ds(k, 1), :] - centre_at) * 4.0
        basis = jnp.where(unit_id < 8, jnp.exp(-offset * offset), 0.0)
        both = jnp.concatenate([basis, -8.0 * offset * basis], axis=1).astype(BF16)
        both = jnp.concatenate([both, jnp.zeros((112, 512), BF16)], axis=0)
        for part in range(4):
            here = slice(part * 256, (part + 1) * 256)
            radial = dot(wrt[here, :], both)
            pre[k, here, :] = radial[:, :256] + dot(wct[here, :], feat_p)
            drad[k, here, :] = radial[:, 256:]
        return carry

    lax.fori_loop(0, SLOTS, before, 0)

    for num in range(8):
        sends[num].wait_send()
        sends[7 - num].wait_recv()
    for pair in range(4):
        tg[:, pair * 2 * GHOSTS : (pair + 1) * 2 * GHOSTS] = jnp.transpose(
            jnp.concatenate([ghost[2 * pair], ghost[2 * pair + 1]], axis=0)
        )

    def mlp(k, sums):
        lanes = pl.ds(pl.multiple_of(k * 256, 256), 256)
        found = dot(tg[...], oh[256:1792, lanes]).astype(BF16) + rows[:, lanes]
        rows[:, lanes] = found
        for part in range(4):
            here = slice(part * 256, (part + 1) * 256)
            act, slope = silu_pair(dot(wnt[here, :], found) + pre[k, here, :])
            act1[here, 0:256] = act.astype(BF16)
            act1[here, 256:512] = (slope * drad[k, here, :]).astype(BF16)
        for part in range(4):
            here = slice(part * 256, (part + 1) * 256)
            hidden = dot(wht[here, :], act1[...])
            act, slope = silu_pair(hidden[:, :256])
            act2[here, 0:256] = act.astype(BF16)
            act2[here, 256:512] = (slope * hidden[:, 256:]).astype(BF16)
        weight = dot(wtt[...], act2[...])
        tws[k] = weight
        unit = [geo[axis, pl.ds(k, 1), :] for axis in range(3)]
        row = found.astype(F32)
        s, v = row[0:CH], [row[CH * (m + 1) : CH * (m + 2)] for m in range(3)]
        w = weight[:, :256] * geo[3, pl.ds(k, 1), :]
        out = [sums[0] + w * (s + unit[0] * v[0] + unit[1] * v[1] + unit[2] * v[2])]
        for m in range(3):
            out.append(sums[m + 1] + w * (s * unit[m] + v[m]))
        return tuple(out)

    sums = lax.fori_loop(
        0, SLOTS, mlp, tuple(jnp.zeros((CH, ATOMS), F32) for _ in range(4))
    )

    eye = iota((CH, CH), 0) == iota((CH, CH), 1)
    read = jnp.sum(jnp.where(eye, ro[...], 0.0), axis=1, keepdims=True)
    inv = sums[0] * sums[0] + sums[1] * sums[1] + sums[2] * sums[2] + sums[3] * sums[3]
    energy = scale * jnp.sum(inv * read, axis=0, keepdims=True) + shift
    factor = 2.0 * scale * read
    cot = [factor * total for total in sums]

    def slopes(k, own):
        lanes = pl.ds(pl.multiple_of(k * 256, 256), 256)
        unit = [geo[axis, pl.ds(k, 1), :] for axis in range(3)]
        env = geo[3, pl.ds(k, 1), :]
        row = rows[:, lanes].astype(F32)
        s, v = row[0:CH], [row[CH * (m + 1) : CH * (m + 2)] for m in range(3)]
        weight = tws[k]
        tw, dtw = weight[:, :256], weight[:, 256:]
        q = cot[0] * (s + unit[0] * v[0] + unit[1] * v[1] + unit[2] * v[2])
        for m in range(3):
            q = q + cot[m + 1] * (s * unit[m] + v[m])
        by_dist = env * jnp.sum(q * dtw, axis=0, keepdims=True)
        by_env = jnp.sum(q * tw, axis=0, keepdims=True)
        w = tw * env
        by_unit = [
            jnp.sum(w * (cot[0] * v[m] + cot[m + 1] * s), axis=0, keepdims=True) for m in range(3)
        ]
        along = by_unit[0] * unit[0] + by_unit[1] * unit[1] + by_unit[2] * unit[2]
        inverse_k = geo[6, pl.ds(k, 1), :]
        common = by_dist - along * inverse_k
        scaled = by_env * geo[5, pl.ds(k, 1), :]
        grad = jnp.concatenate(
            [
                common * unit[m] + scaled * dsp[m, pl.ds(k, 1), :] + by_unit[m] * inverse_k
                for m in range(3)
            ]
            + [jnp.zeros((5, ATOMS), F32)],
            axis=0,
        )
        high, low = split(grad)
        grads[0:8, lanes] = high
        grads[8:16, lanes] = low
        return own + grad

    own = lax.fori_loop(0, SLOTS, slopes, jnp.zeros((8, ATOMS), F32))

    def scatter(first, size):
        both = lax.dot_general(
            grads[...],
            oh[first : first + size, :],
            (((1,), (1,)), ((), ())),
            preferred_element_type=F32,
        )
        return both[0:8] + both[8:16]

    returns = []
    for num in range(8):
        back_out[num] = scatter(ATOMS + num * GHOSTS, GHOSTS)
        copy = pltpu.make_async_remote_copy(
            src_ref=back_out.at[num],
            dst_ref=back_in.at[7 - num],
            send_sem=bsend_sem.at[num],
            recv_sem=brecv_sem.at[7 - num],
            device_id=peers[num],
            device_id_type=MESH,
        )
        copy.start()
        returns.append(copy)
    tail = jnp.concatenate([own[0:3], energy, jnp.zeros((4, ATOMS), F32)], axis=0)
    tail = jnp.dot(
        tail, jnp.where(swap, 1.0, 0.0), preferred_element_type=F32, precision=lax.Precision.HIGHEST
    )
    en_ref[...] = tail[3:4]
    total = tail[0:3] - scatter(0, ATOMS)[0:3]
    for num in range(8):
        returns[num].wait_send()
        returns[7 - num].wait_recv()
    for num in range(8):
        high, low = split(back_in[num])
        landed = dot(jnp.concatenate([high, low], axis=0), sel[num])
        total = total + landed[0:3] + landed[8:11]
    fo_ref[...] = total


def shards(
    features,
    displacement,
    neighbours,
    neighbour_count,
    species,
    send_list,
    send_count,
    w_center,
    w_neighbour,
    w_radial,
    w_hidden,
    w_tensor,
    readout,
    species_scale,
    species_shift,
):
    vmem = pl.BlockSpec(memory_space=pltpu.VMEM)
    hbm = pl.BlockSpec(memory_space=pl.ANY)
    energy, forces = pl.pallas_call(
        kernel,
        out_shape=(
            jax.ShapeDtypeStruct((1, ATOMS), F32),
            jax.ShapeDtypeStruct((3, ATOMS), F32),
        ),
        in_specs=[vmem] * 7 + [hbm, hbm, vmem, hbm, hbm] + [vmem] * 3,
        out_specs=(vmem, vmem),
        scratch_shapes=[
            pltpu.VMEM((WIDTH, HID), BF16),
            pltpu.VMEM((WIDTH, HID), BF16),
            pltpu.VMEM((HID, HID), BF16),
            pltpu.VMEM((HID, CH), BF16),
            pltpu.VMEM((HID, WIDTH), BF16),
            pltpu.VMEM((HID, WIDTH), BF16),
            pltpu.VMEM((HID, 128), BF16),
            pltpu.VMEM((HID, HID), BF16),
            pltpu.VMEM((CH, HID), BF16),
            pltpu.VMEM((8, GHOSTS, ATOMS), BF16),
            pltpu.VMEM((8, GHOSTS, WIDTH), BF16),
            pltpu.VMEM((8, GHOSTS, WIDTH), BF16),
            pltpu.VMEM((WIDTH, 8 * GHOSTS), BF16),
            pltpu.VMEM((64, 128), F32),
            pltpu.VMEM((4, SLOTS, ATOMS), F32),
            pltpu.VMEM((7, SLOTS, ATOMS), F32),
            pltpu.VMEM((ATOMS + 8 * GHOSTS, EDGES), BF16),
            pltpu.VMEM((SLOTS, HID, ATOMS), F32),
            pltpu.VMEM((SLOTS, HID, ATOMS), F32),
            pltpu.VMEM((WIDTH, EDGES), BF16),
            pltpu.VMEM((HID, 2 * ATOMS), BF16),
            pltpu.VMEM((HID, 2 * ATOMS), BF16),
            pltpu.VMEM((SLOTS, CH, 2 * ATOMS), F32),
            pltpu.VMEM((16, EDGES), BF16),
            pltpu.VMEM((8, 8, GHOSTS), F32),
            pltpu.VMEM((8, 8, GHOSTS), F32),
            pltpu.SemaphoreType.DMA((4,)),
            pltpu.SemaphoreType.DMA((8,)),
            pltpu.SemaphoreType.DMA((8,)),
            pltpu.SemaphoreType.DMA((8,)),
            pltpu.SemaphoreType.DMA((8,)),
        ],
        compiler_params=pltpu.CompilerParams(
            collective_id=0, has_side_effects=True, vmem_limit_bytes=56 * 1024 * 1024
        ),
        cost_estimate=pl.CostEstimate(
            flops=14_000_000_000, bytes_accessed=4_000_000, transcendentals=4_000_000
        ),
    )(
        features[0, 0],
        displacement[0, 0],
        neighbours[0],
        neighbour_count[0],
        species[0],
        send_list[0, 0],
        send_count[0],
        w_center,
        w_neighbour,
        w_radial,
        w_hidden,
        w_tensor,
        readout[None],
        species_scale[None],
        species_shift[None],
    )
    return energy[None], forces[None, None]


def solution(mesh):
    placed = (
        P("gx", "gy", None, None),
        P("gx", "gy", None, None),
        P("gx", "gy", None),
        P("gx", "gy", None),
        P("gx", "gy", None),
        P("gx", "gy", None, None),
        P("gx", "gy", None),
        P(),
        P(),
        P(),
        P(),
        P(),
        P(),
        P(),
        P(),
    )
    return jax.shard_map(
        shards,
        mesh=mesh,
        in_specs=placed,
        out_specs=(P("gx", "gy", None), P("gx", "gy", None, None)),
        check_vma=False,
    )
```

time: 174 us -> 58 us (0.33)
  the two profiles are of different devices: /device:TPU:2 before, /device:TPU:8 now
where the time goes in v1:
time: 58 us; the launch traced here: 57.8 us
  Pallas kernels  51.5 us (89%)
  local copies, waits for them, and re-layouts  5.59 us (10%)
  between operations  0.64 us (1%)
    pallas_call x1, Pallas kernels, shards(): pl.pallas_call(kernel, out_shape=(jax.ShapeDtypeStruct((1, ATOMS), F32),...  51.5 us
    unnamed x4, local copies, waits for them, and re-layouts  5.59 us

profile of v1, /device:TPU:8, one launch (start us, length us, event | category | flops | bytes accessed | tf_op | source)
XLA Modules:
  0.0 57.8 jit_solution(5782240305867179254)
XLA Ops:
  0.6 1.4 %copy.21 = f32[1,1,3,2048]{3,2,1,0:T(4,128)} copy(f32[1,1,3,2048]{3,1,2,0:T(1,128)} %param.16) | data formatting | bytes 49152
  2.0 1.7 %copy.17.wt_hbm = bf16[1024,64]{1,0:T(8,128)(2,1)} copy(bf16[1024,64]{0,1:T(8,128)(2,1)} %param.26) | data formatting | bytes 262144 | tf_op args[11]
  3.7 51.5 %shard_map.158 = (f32[1,256]{1,0:T(1,128)}, f32[3,256]{1,0:T(4,128)}) custom-call(bf16[256,256]{1,0:T(8,128)(2,1)} %bitcast.17, f32[3,2048]{1,0:T(4,128)} %bitcast.14, s32[1,2048]{1,0:T(1,128)} %bitcast.18, s32[1,256]{1,0:T(1,128)} %bitcast.20, s32[1,256]{1,0:T(1,128)} %bitcast.21, s32[8,192]{1,0:T(8,128)} %bitcast.19, s32[1,8]{1,0:T(1,128)} %bitcast.22, ...), custom_call_target="tpu_custom_call" | custom-call | flops 14000000000 | bytes 4000000 | tf_op jit(solution)/shard_map/pallas_call | solution.py:356
  55.3 1.3 %copy.18 = f32[1,1,3,256]{3,1,2,0:T(1,128)} copy(f32[1,1,3,256]{3,2,1,0:T(4,128)} %bitcast.15) | data formatting | bytes 6144
  56.5 1.2 %copy.23 = f32[1,1,256]{2,1,0:T(1,128)} copy(f32[1,1,256]{2,1,0:T(1,128)} %bitcast.16) | data formatting | bytes 2048

commit v2 on v1

--- a/solution.py
+++ b/solution.py
@@ -53,16 +53,14 @@
     wn_hbm,
     wr,
     wh_hbm,
-    wt_hbm,
+    wtt_hbm,
     ro,
     sscale,
     sshift,
-    en_ref,
-    fo_ref,
+    out_ref,
     wc,
     wn,
     wh,
-    wt,
     wct,
     wnt,
     wrt,
@@ -71,7 +69,6 @@
     sel,
     outg,
     ghost,
-    tg,
     stage,
     dsp,
     geo,
@@ -82,7 +79,6 @@
     act1,
     act2,
     tws,
-    grads,
     back_out,
     back_in,
     load_sem,
@@ -93,20 +89,33 @@
 ):
     px, qy = lax.axis_index("gx"), lax.axis_index("gy")
     nx, ny = lax.axis_size("gx"), lax.axis_size("gy")
-    peers = [
-        (lax.rem(px + (ox + nx), nx), lax.rem(qy + (oy + ny), ny)) for ox, oy in DIRECTIONS
+
+    def peer(ox, oy):
+        return lax.rem(px + (ox + nx), nx), lax.rem(qy + (oy + ny), ny)
+
+    core = lax.rem(qy, 2)
+    side = 2 * core - 1
+    order = [
+        (6 + side, peer(1, side)),
+        (1 + side, peer(-1, side)),
+        (3 + core, peer(0, side)),
+        (6 - side, peer(1, -side)),
+        (1 - side, peer(-1, -side)),
+        (6, peer(1, 0)),
+        (1, peer(-1, 0)),
+        (4 - core, peer(0, -side)),
     ]
     loads = [
         pltpu.make_async_copy(src, dst, load_sem.at[num])
         for num, (src, dst) in enumerate(
-            ((wc_hbm, wc), (wn_hbm, wn), (wh_hbm, wh), (wt_hbm, wt))
+            ((wc_hbm, wc), (wn_hbm, wn), (wh_hbm, wh), (wtt_hbm, wtt))
         )
     ]
     for load in loads:
         load.start()
     barrier = pltpu.get_barrier_semaphore()
-    for peer in peers:
-        pl.semaphore_signal(barrier, inc=1, device_id=peer, device_id_type=MESH)
+    for _, device in order:
+        pl.semaphore_signal(barrier, inc=1, device_id=device, device_id_type=MESH)
 
     kept = jnp.where(
         iota((GHOSTS, 8), 0) < scnt[...], jnp.transpose(lists[...].astype(F32)), -1.0
@@ -118,13 +127,13 @@
         outg[num] = dot(hit, feat[...]).astype(BF16)
     pl.semaphore_wait(barrier, 8)
     sends = []
-    for num in range(8):
+    for num, peer in order:
         copy = pltpu.make_async_remote_copy(
             src_ref=outg.at[num],
             dst_ref=ghost.at[7 - num],
             send_sem=send_sem.at[num],
             recv_sem=recv_sem.at[7 - num],
-            device_id=peers[num],
+            device_id=peer,
             device_id_type=MESH,
         )
         copy.start()
@@ -132,7 +141,7 @@
 
     for axis in range(3):
         for c in range(16):
-            stage[pl.ds(axis * 16 + c, 1), :] = disp[axis : axis + 1, c * 128 : (c + 1) * 128]
+            stage[pl.ds(axis * 16 + c, 1), :] = disp[axis, :, c * 128 : (c + 1) * 128]
     for c in range(16):
         stage[pl.ds(48 + c, 1), :] = nbr[0:1, c * 128 : (c + 1) * 128].astype(F32)
     turned = jnp.transpose(stage[...])
@@ -187,8 +196,6 @@
 
     lax.fori_loop(0, 4, turn, 0)
     loads[3].wait()
-    for part in range(4):
-        wtt[:, part * 256 : (part + 1) * 256] = jnp.transpose(wt[part * 256 : (part + 1) * 256, :])
 
     feat_t = jnp.transpose(feat[...])
     feat_p = dot(feat_t, swap_b).astype(BF16)
@@ -215,18 +222,23 @@
 
     lax.fori_loop(0, SLOTS, before, 0)
 
-    for num in range(8):
-        sends[num].wait_send()
-        sends[7 - num].wait_recv()
-    for pair in range(4):
-        tg[:, pair * 2 * GHOSTS : (pair + 1) * 2 * GHOSTS] = jnp.transpose(
-            jnp.concatenate([ghost[2 * pair], ghost[2 * pair + 1]], axis=0)
-        )
+    def take(num):
+        turned = jnp.transpose(ghost[num])
+        first = pl.multiple_of(ATOMS + num * GHOSTS, 64)
+        for part in range(4):
+            here = slice(part * 512, (part + 1) * 512)
+            found = dot(turned, oh[pl.ds(first, GHOSTS), here])
+            rows[:, here] = rows[:, here] + found.astype(BF16)
+
+    for copy in sends:
+        copy.wait_send()
+    for copy in (2, 5, 6, 1, 0, 7, 4, 3):
+        sends[copy].wait_recv()
+        take(7 - order[copy][0])
 
     def mlp(k, sums):
-        lanes = pl.ds(pl.multiple_of(k * 256, 256), 256)
-        found = dot(tg[...], oh[256:1792, lanes]).astype(BF16) + rows[:, lanes]
-        rows[:, lanes] = found
+        lanes = slice(k * 256, (k + 1) * 256)
+        found = rows[:, lanes]
         for part in range(4):
             here = slice(part * 256, (part + 1) * 256)
             act, slope = silu_pair(dot(wnt[here, :], found) + pre[k, here, :])
@@ -249,9 +261,9 @@
             out.append(sums[m + 1] + w * (s * unit[m] + v[m]))
         return tuple(out)
 
-    sums = lax.fori_loop(
-        0, SLOTS, mlp, tuple(jnp.zeros((CH, ATOMS), F32) for _ in range(4))
-    )
+    sums = tuple(jnp.zeros((CH, ATOMS), F32) for _ in range(4))
+    for k in range(SLOTS):
+        sums = mlp(k, sums)
 
     eye = iota((CH, CH), 0) == iota((CH, CH), 1)
     read = jnp.sum(jnp.where(eye, ro[...], 0.0), axis=1, keepdims=True)
@@ -260,8 +272,8 @@
     factor = 2.0 * scale * read
     cot = [factor * total for total in sums]
 
-    def slopes(k, own):
-        lanes = pl.ds(pl.multiple_of(k * 256, 256), 256)
+    def slopes(k, own, landed):
+        lanes = slice(k * 256, (k + 1) * 256)
         unit = [geo[axis, pl.ds(k, 1), :] for axis in range(3)]
         env = geo[3, pl.ds(k, 1), :]
         row = rows[:, lanes].astype(F32)
@@ -289,31 +301,30 @@
             + [jnp.zeros((5, ATOMS), F32)],
             axis=0,
         )
-        high, low = split(grad)
-        grads[0:8, lanes] = high
-        grads[8:16, lanes] = low
-        return own + grad
-
-    own = lax.fori_loop(0, SLOTS, slopes, jnp.zeros((8, ATOMS), F32))
-
-    def scatter(first, size):
-        both = lax.dot_general(
-            grads[...],
-            oh[first : first + size, :],
+        spread = lax.dot_general(
+            jnp.concatenate(split(grad), axis=0),
+            oh[:, lanes],
             (((1,), (1,)), ((), ())),
             preferred_element_type=F32,
         )
-        return both[0:8] + both[8:16]
-
+        return own + grad, landed + spread
+
+    own = jnp.zeros((8, ATOMS), F32)
+    landed = jnp.zeros((16, ATOMS + 8 * GHOSTS), F32)
+    for k in range(SLOTS):
+        own, landed = slopes(k, own, landed)
+    landed = landed[0:8] + landed[8:16]
+
+    for num in range(8):
+        back_out[num] = landed[:, ATOMS + num * GHOSTS : ATOMS + (num + 1) * GHOSTS]
     returns = []
-    for num in range(8):
-        back_out[num] = scatter(ATOMS + num * GHOSTS, GHOSTS)
+    for num, device in order:
         copy = pltpu.make_async_remote_copy(
             src_ref=back_out.at[num],
             dst_ref=back_in.at[7 - num],
             send_sem=bsend_sem.at[num],
             recv_sem=brecv_sem.at[7 - num],
-            device_id=peers[num],
+            device_id=device,
             device_id_type=MESH,
         )
         copy.start()
@@ -322,16 +333,21 @@
     tail = jnp.dot(
         tail, jnp.where(swap, 1.0, 0.0), preferred_element_type=F32, precision=lax.Precision.HIGHEST
     )
-    en_ref[...] = tail[3:4]
-    total = tail[0:3] - scatter(0, ATOMS)[0:3]
-    for num in range(8):
-        returns[num].wait_send()
-        returns[7 - num].wait_recv()
-    for num in range(8):
-        high, low = split(back_in[num])
-        landed = dot(jnp.concatenate([high, low], axis=0), sel[num])
-        total = total + landed[0:3] + landed[8:11]
-    fo_ref[...] = total
+    total = tail[0:3] - landed[0:3, 0:ATOMS]
+    for copy in returns:
+        copy.wait_send()
+    for copy in (2, 5, 6, 1, 0, 7, 4, 3):
+        returns[copy].wait_recv()
+        num = 7 - order[copy][0]
+        both = dot(jnp.concatenate(split(back_in[num]), axis=0), sel[num])
+        total = total + both[0:3] + both[8:11]
+    out_ref[...] = jnp.concatenate([total, tail[3:4]], axis=0)
+
+
+def hand_over(both, en_ref, fo_ref):
+    en_ref[...] = both[3:4]
+    for axis in range(3):
+        fo_ref[axis] = both[axis : axis + 1]
 
 
 def shards(
@@ -353,19 +369,15 @@
 ):
     vmem = pl.BlockSpec(memory_space=pltpu.VMEM)
     hbm = pl.BlockSpec(memory_space=pl.ANY)
-    energy, forces = pl.pallas_call(
+    both = pl.pallas_call(
         kernel,
-        out_shape=(
-            jax.ShapeDtypeStruct((1, ATOMS), F32),
-            jax.ShapeDtypeStruct((3, ATOMS), F32),
-        ),
+        out_shape=jax.ShapeDtypeStruct((4, ATOMS), F32),
         in_specs=[vmem] * 7 + [hbm, hbm, vmem, hbm, hbm] + [vmem] * 3,
-        out_specs=(vmem, vmem),
+        out_specs=vmem,
         scratch_shapes=[
             pltpu.VMEM((WIDTH, HID), BF16),
             pltpu.VMEM((WIDTH, HID), BF16),
             pltpu.VMEM((HID, HID), BF16),
-            pltpu.VMEM((HID, CH), BF16),
             pltpu.VMEM((HID, WIDTH), BF16),
             pltpu.VMEM((HID, WIDTH), BF16),
             pltpu.VMEM((HID, 128), BF16),
@@ -374,7 +386,6 @@
             pltpu.VMEM((8, GHOSTS, ATOMS), BF16),
             pltpu.VMEM((8, GHOSTS, WIDTH), BF16),
             pltpu.VMEM((8, GHOSTS, WIDTH), BF16),
-            pltpu.VMEM((WIDTH, 8 * GHOSTS), BF16),
             pltpu.VMEM((64, 128), F32),
             pltpu.VMEM((4, SLOTS, ATOMS), F32),
             pltpu.VMEM((7, SLOTS, ATOMS), F32),
@@ -385,7 +396,6 @@
             pltpu.VMEM((HID, 2 * ATOMS), BF16),
             pltpu.VMEM((HID, 2 * ATOMS), BF16),
             pltpu.VMEM((SLOTS, CH, 2 * ATOMS), F32),
-            pltpu.VMEM((16, EDGES), BF16),
             pltpu.VMEM((8, 8, GHOSTS), F32),
             pltpu.VMEM((8, 8, GHOSTS), F32),
             pltpu.SemaphoreType.DMA((4,)),
@@ -402,7 +412,7 @@
         ),
     )(
         features[0, 0],
-        displacement[0, 0],
+        displacement.reshape(3, 1, EDGES),
         neighbours[0],
         neighbour_count[0],
         species[0],
@@ -412,12 +422,21 @@
         w_neighbour,
         w_radial,
         w_hidden,
-        w_tensor,
+        w_tensor.T,
         readout[None],
         species_scale[None],
         species_shift[None],
     )
-    return energy[None], forces[None, None]
+    energy, forces = pl.pallas_call(
+        hand_over,
+        out_shape=(
+            jax.ShapeDtypeStruct((1, ATOMS), F32),
+            jax.ShapeDtypeStruct((3, 1, ATOMS), F32),
+        ),
+        in_specs=[vmem],
+        out_specs=(vmem, vmem),
+    )(both)
+    return energy[None], forces.reshape(1, 1, 3, ATOMS)
 
 
 def solution(mesh):

time: 58 us -> 48.6 us (0.84)
  the two profiles are of different devices: /device:TPU:8 before, /device:TPU:1 now
where the time goes in v2:
time: 48.6 us; the launch traced here: 48.5 us
  Pallas kernels  47.8 us (98%)
  between operations  0.64 us (1%)
    pallas_call x1, Pallas kernels, shards(): pl.pallas_call(kernel, out_shape=jax.ShapeDtypeStruct((4, ATOMS), F32), i...  46.6 us
    pallas_call x1, Pallas kernels, shards(): pl.pallas_call(hand_over, out_shape=(jax.ShapeDtypeStruct((1, ATOMS), F32...  1.26 us

profile of v2, /device:TPU:1, one launch (start us, length us, event | category | flops | bytes accessed | tf_op | source)
XLA Modules:
  0.0 48.5 jit_solution(10320204320534615121)
XLA Ops:
  0.6 46.6 %shard_map.158.both = f32[4,256]{1,0:T(4,128)} custom-call(bf16[256,256]{1,0:T(8,128)(2,1)} %bitcast.15, f32[3,1,2048]{2,1,0:T(1,128)} %bitcast.17, s32[1,2048]{1,0:T(1,128)} %bitcast.18, s32[1,256]{1,0:T(1,128)} %bitcast.21, s32[1,256]{1,0:T(1,128)} %bitcast.22, s32[8,192]{1,0:T(8,128)} %bitcast.19, s32[1,8]{1,0:T(1,128)} %bitcast.24, ...), custom_call_target="tpu_custom_call" | custom-call | flops 14000000000 | bytes 4000000 | tf_op jit(solution)/shard_map/pallas_call | solution.py:372
  47.2 1.3 %shard_map.159 = (f32[1,256]{1,0:T(1,128)}, f32[3,1,256]{2,1,0:T(1,128)}) custom-call(f32[4,256]{1,0:T(4,128)} %shard_map.158.both), custom_call_target="tpu_custom_call" | custom-call | tf_op jit(solution)/shard_map/pallas_call | solution.py:430

commit v3 on v2

--- a/solution.py
+++ b/solution.py
@@ -42,6 +42,22 @@
 
 
 def kernel(
+    feat_hbm,
+    disp_hbm,
+    nbr_hbm,
+    cnt_hbm,
+    spc_hbm,
+    lists_hbm,
+    scnt_hbm,
+    wc_hbm,
+    wn_hbm,
+    wr_hbm,
+    wh_hbm,
+    wtt_hbm,
+    ro_hbm,
+    sscale_hbm,
+    sshift_hbm,
+    out_ref,
     feat,
     disp,
     nbr,
@@ -49,15 +65,10 @@
     spc,
     lists,
     scnt,
-    wc_hbm,
-    wn_hbm,
     wr,
-    wh_hbm,
-    wtt_hbm,
     ro,
     sscale,
     sshift,
-    out_ref,
     wc,
     wn,
     wh,
@@ -73,6 +84,8 @@
     dsp,
     geo,
     oh,
+    low_hot,
+    high_hot,
     pre,
     drad,
     rows,
@@ -105,26 +118,46 @@
         (1, peer(-1, 0)),
         (4 - core, peer(0, -side)),
     ]
+    barrier = pltpu.get_barrier_semaphore()
+    for _, device in order:
+        pl.semaphore_signal(barrier, inc=1, device_id=device, device_id_type=MESH)
+
+    pairs = (
+        (lists_hbm, lists),
+        (scnt_hbm, scnt),
+        (feat_hbm, feat),
+        (disp_hbm, disp),
+        (nbr_hbm, nbr),
+        (cnt_hbm, cnt),
+        (spc_hbm, spc),
+        (sscale_hbm, sscale),
+        (sshift_hbm, sshift),
+        (ro_hbm, ro),
+        (wr_hbm, wr),
+        (wc_hbm, wc),
+        (wn_hbm, wn),
+        (wh_hbm, wh),
+        (wtt_hbm, wtt),
+    )
     loads = [
-        pltpu.make_async_copy(src, dst, load_sem.at[num])
-        for num, (src, dst) in enumerate(
-            ((wc_hbm, wc), (wn_hbm, wn), (wh_hbm, wh), (wtt_hbm, wtt))
-        )
+        pltpu.make_async_copy(src, dst, load_sem.at[num]) for num, (src, dst) in enumerate(pairs)
     ]
     for load in loads:
         load.start()
-    barrier = pltpu.get_barrier_semaphore()
-    for _, device in order:
-        pl.semaphore_signal(barrier, inc=1, device_id=device, device_id_type=MESH)
-
-    kept = jnp.where(
-        iota((GHOSTS, 8), 0) < scnt[...], jnp.transpose(lists[...].astype(F32)), -1.0
-    )
-    lane = iota((GHOSTS, ATOMS), 1).astype(F32)
+    for load in loads[0:3]:
+        load.wait()
+
+    ids = jnp.concatenate([lists[...].astype(F32), jnp.zeros((8, ATOMS - GHOSTS), F32)], axis=1)
+    slot = iota((ATOMS, 8), 0)
+    kept = jnp.where((slot < scnt[...]) & (slot < GHOSTS), jnp.transpose(ids), -1.0)
+    lane = iota((ATOMS, ATOMS), 1).astype(F32)
     for num in range(8):
         hit = one_hot(kept[:, num : num + 1] == lane)
-        sel[num] = hit
-        outg[num] = dot(hit, feat[...]).astype(BF16)
+        for half in range(2):
+            sel[num * 128 : (num + 1) * 128, half * 256 : (half + 1) * 256] = hit[
+                half * 128 : (half + 1) * 128
+            ]
+        outg[num] = dot(hit[0:GHOSTS], feat[...]).astype(BF16)
     pl.semaphore_wait(barrier, 8)
     sends = []
     for num, peer in order:
@@ -138,6 +171,9 @@
         )
         copy.start()
         sends.append(copy)
+
+    for load in loads[3:11]:
+        load.wait()
 
     for axis in range(3):
         for c in range(16):
@@ -178,13 +214,13 @@
     wrt[...] = jnp.transpose(
         jnp.concatenate([wr[...].astype(F32), jnp.zeros((120, HID), F32)], axis=0)
     ).astype(BF16)
-    loads[0].wait()
+    loads[11].wait()
     for num in range(4):
         wct[num * 256 : (num + 1) * 256, :] = jnp.transpose(wc[:, num * 256 : (num + 1) * 256])
-    loads[1].wait()
+    loads[12].wait()
     for num in range(4):
         wnt[num * 256 : (num + 1) * 256, :] = jnp.transpose(wn[:, num * 256 : (num + 1) * 256])
-    loads[2].wait()
+    loads[13].wait()
 
     def turn(num, carry):
         start = pl.multiple_of(num * 256, 256)
@@ -195,7 +231,7 @@
         return carry
 
     lax.fori_loop(0, 4, turn, 0)
-    loads[3].wait()
+    loads[14].wait()
 
     feat_t = jnp.transpose(feat[...])
     feat_p = dot(feat_t, swap_b).astype(BF16)
@@ -209,6 +245,15 @@
         for part in range(7):
             oh[part * 256 : (part + 1) * 256, lanes] = one_hot(row_id + (part * 256.0) == ids)
         rows[:, lanes] = dot(feat_t, oh[0:256, lanes]).astype(BF16)
+        own = ids < float(ATOMS)
+        block = jnp.zeros((1, ATOMS), F32)
+        for num in range(1, 8):
+            block = block + jnp.where(ids >= float(ATOMS + num * GHOSTS), 1.0, 0.0)
+        inside = jnp.where(own, ids, ids - float(ATOMS) - block * float(GHOSTS))
+        upper = jnp.where(inside >= 128.0, 1.0, 0.0)
+        low_hot[:, lanes] = one_hot(row_id[0:128] == inside - 128.0 * upper)
+        part_id = jnp.where(own, 16.0, 2.0 * block) + upper
+        high_hot[:, lanes] = one_hot(row_id[0:32] == part_id)
         offset = (geo[4, pl.ds(k, 1), :] - centre_at) * 4.0
         basis = jnp.where(unit_id < 8, jnp.exp(-offset * offset), 0.0)
         both = jnp.concatenate([basis, -8.0 * offset * basis], axis=1).astype(BF16)
@@ -236,34 +281,42 @@
         sends[copy].wait_recv()
         take(7 - order[copy][0])
 
-    def mlp(k, sums):
-        lanes = slice(k * 256, (k + 1) * 256)
-        found = rows[:, lanes]
+    def first(k, at):
+        found = rows[:, k * 256 : (k + 1) * 256]
         for part in range(4):
             here = slice(part * 256, (part + 1) * 256)
             act, slope = silu_pair(dot(wnt[here, :], found) + pre[k, here, :])
-            act1[here, 0:256] = act.astype(BF16)
-            act1[here, 256:512] = (slope * drad[k, here, :]).astype(BF16)
+            act1[here, at : at + 256] = act.astype(BF16)
+            act1[here, at + 256 : at + 512] = (slope * drad[k, here, :]).astype(BF16)
+
+    def second(at):
         for part in range(4):
             here = slice(part * 256, (part + 1) * 256)
-            hidden = dot(wht[here, :], act1[...])
+            hidden = dot(wht[here, :], act1[:, at : at + 512])
             act, slope = silu_pair(hidden[:, :256])
-            act2[here, 0:256] = act.astype(BF16)
-            act2[here, 256:512] = (slope * hidden[:, 256:]).astype(BF16)
-        weight = dot(wtt[...], act2[...])
+            act2[here, at : at + 256] = act.astype(BF16)
+            act2[here, at + 256 : at + 512] = (slope * hidden[:, 256:]).astype(BF16)
+
+    def product(k, weight, sums):
         tws[k] = weight
-        unit = [geo[axis, pl.ds(k, 1), :] for axis in range(3)]
-        row = found.astype(F32)
+        unit = [geo[axis, k : k + 1, :] for axis in range(3)]
+        row = rows[:, k * 256 : (k + 1) * 256].astype(F32)
         s, v = row[0:CH], [row[CH * (m + 1) : CH * (m + 2)] for m in range(3)]
-        w = weight[:, :256] * geo[3, pl.ds(k, 1), :]
+        w = weight[:, :256] * geo[3, k : k + 1, :]
         out = [sums[0] + w * (s + unit[0] * v[0] + unit[1] * v[1] + unit[2] * v[2])]
         for m in range(3):
             out.append(sums[m + 1] + w * (s * unit[m] + v[m]))
         return tuple(out)
 
     sums = tuple(jnp.zeros((CH, ATOMS), F32) for _ in range(4))
-    for k in range(SLOTS):
-        sums = mlp(k, sums)
+    for k in range(0, SLOTS, 2):
+        first(k, 0)
+        first(k + 1, 512)
+        second(0)
+        second(512)
+        weight = dot(wtt[...], act2[...])
+        sums = product(k, weight[:, 0:512], sums)
+        sums = product(k + 1, weight[:, 512:], sums)
 
     eye = iota((CH, CH), 0) == iota((CH, CH), 1)
     read = jnp.sum(jnp.where(eye, ro[...], 0.0), axis=1, keepdims=True)
@@ -301,22 +354,28 @@
             + [jnp.zeros((5, ATOMS), F32)],
             axis=0,
         )
+        high, low = split(grad[0:3])
+        flat = jnp.concatenate([high, low], axis=0)
         spread = lax.dot_general(
-            jnp.concatenate(split(grad), axis=0),
-            oh[:, lanes],
+            jnp.concatenate([high_hot[:, lanes] * flat[m : m + 1] for m in range(6)], axis=0),
+            low_hot[:, lanes],
             (((1,), (1,)), ((), ())),
             preferred_element_type=F32,
         )
         return own + grad, landed + spread
 
     own = jnp.zeros((8, ATOMS), F32)
-    landed = jnp.zeros((16, ATOMS + 8 * GHOSTS), F32)
+    landed = jnp.zeros((192, 128), F32)
     for k in range(SLOTS):
         own, landed = slopes(k, own, landed)
-    landed = landed[0:8] + landed[8:16]
-
+    landed = landed[0:96] + landed[96:192]
     for num in range(8):
-        back_out[num] = landed[:, ATOMS + num * GHOSTS : ATOMS + (num + 1) * GHOSTS]
+        pair = [landed[m * 32 + 2 * num : m * 32 + 2 * num + 2] for m in range(3)]
+        none = jnp.zeros((1, 128), F32)
+        back_out[num] = jnp.concatenate(
+            [side_row for half in range(2) for side_row in [p[half : half + 1] for p in pair] + [none]],
+            axis=0,
+        )
     returns = []
     for num, device in order:
         copy = pltpu.make_async_remote_copy(
@@ -333,21 +392,33 @@
     tail = jnp.dot(
         tail, jnp.where(swap, 1.0, 0.0), preferred_element_type=F32, precision=lax.Precision.HIGHEST
     )
-    total = tail[0:3] - landed[0:3, 0:ATOMS]
+    total = tail[0:3] - jnp.concatenate(
+        [
+            jnp.concatenate([landed[m * 32 + 16 + half : m * 32 + 17 + half] for m in range(3)], axis=0)
+            for half in range(2)
+        ],
+        axis=1,
+    )
+    for copy in returns:
+        copy.wait_recv()
+    back = jnp.concatenate([back_in[num] for num in range(8)], axis=1)
+    both = dot(jnp.concatenate(split(back), axis=0), sel[...])
+    both = both[0:8] + both[8:16]
+    total = total + both[0:3, 0:ATOMS] + both[4:7, ATOMS:]
     for copy in returns:
         copy.wait_send()
-    for copy in (2, 5, 6, 1, 0, 7, 4, 3):
-        returns[copy].wait_recv()
-        num = 7 - order[copy][0]
-        both = dot(jnp.concatenate(split(back_in[num]), axis=0), sel[num])
-        total = total + both[0:3] + both[8:11]
-    out_ref[...] = jnp.concatenate([total, tail[3:4]], axis=0)
-
-
-def hand_over(both, en_ref, fo_ref):
-    en_ref[...] = both[3:4]
     for axis in range(3):
-        fo_ref[axis] = both[axis : axis + 1]
+        out_ref[axis] = total[axis : axis + 1]
+    out_ref[3] = tail[3:4]
+
+
+def hand_over(both, en_ref, fo_ref, sem):
+    energy = pltpu.make_async_copy(both.at[3], en_ref, sem.at[0])
+    forces = pltpu.make_async_copy(both.at[pl.ds(0, 3)], fo_ref, sem.at[1])
+    energy.start()
+    forces.start()
+    energy.wait()
+    forces.wait()
 
 
 def shards(
@@ -371,10 +442,21 @@
     hbm = pl.BlockSpec(memory_space=pl.ANY)
     both = pl.pallas_call(
         kernel,
-        out_shape=jax.ShapeDtypeStruct((4, ATOMS), F32),
-        in_specs=[vmem] * 7 + [hbm, hbm, vmem, hbm, hbm] + [vmem] * 3,
+        out_shape=jax.ShapeDtypeStruct((4, 1, ATOMS), F32),
+        in_specs=[hbm] * 15,
         out_specs=vmem,
         scratch_shapes=[
+            pltpu.VMEM((ATOMS, WIDTH), BF16),
+            pltpu.VMEM((3, 1, EDGES), F32),
+            pltpu.VMEM((1, EDGES), jnp.int32),
+            pltpu.VMEM((1, ATOMS), jnp.int32),
+            pltpu.VMEM((1, ATOMS), jnp.int32),
+            pltpu.VMEM((8, GHOSTS), jnp.int32),
+            pltpu.VMEM((1, 8), jnp.int32),
+            pltpu.VMEM((8, HID), BF16),
+            pltpu.VMEM((1, CH), F32),
+            pltpu.VMEM((1, 4), F32),
+            pltpu.VMEM((1, 4), F32),
             pltpu.VMEM((WIDTH, HID), BF16),
             pltpu.VMEM((WIDTH, HID), BF16),
             pltpu.VMEM((HID, HID), BF16),
@@ -383,22 +465,24 @@
             pltpu.VMEM((HID, 128), BF16),
             pltpu.VMEM((HID, HID), BF16),
             pltpu.VMEM((CH, HID), BF16),
-            pltpu.VMEM((8, GHOSTS, ATOMS), BF16),
+            pltpu.VMEM((8 * 128, 2 * ATOMS), BF16),
             pltpu.VMEM((8, GHOSTS, WIDTH), BF16),
             pltpu.VMEM((8, GHOSTS, WIDTH), BF16),
             pltpu.VMEM((64, 128), F32),
             pltpu.VMEM((4, SLOTS, ATOMS), F32),
             pltpu.VMEM((7, SLOTS, ATOMS), F32),
             pltpu.VMEM((ATOMS + 8 * GHOSTS, EDGES), BF16),
+            pltpu.VMEM((128, EDGES), BF16),
+            pltpu.VMEM((32, EDGES), BF16),
             pltpu.VMEM((SLOTS, HID, ATOMS), F32),
             pltpu.VMEM((SLOTS, HID, ATOMS), F32),
             pltpu.VMEM((WIDTH, EDGES), BF16),
-            pltpu.VMEM((HID, 2 * ATOMS), BF16),
-            pltpu.VMEM((HID, 2 * ATOMS), BF16),
+            pltpu.VMEM((HID, 4 * ATOMS), BF16),
+            pltpu.VMEM((HID, 4 * ATOMS), BF16),
             pltpu.VMEM((SLOTS, CH, 2 * ATOMS), F32),
-            pltpu.VMEM((8, 8, GHOSTS), F32),
-            pltpu.VMEM((8, 8, GHOSTS), F32),
-            pltpu.SemaphoreType.DMA((4,)),
+            pltpu.VMEM((8, 8, 128), F32),
+            pltpu.VMEM((8, 8, 128), F32),
+            pltpu.SemaphoreType.DMA((15,)),
             pltpu.SemaphoreType.DMA((8,)),
             pltpu.SemaphoreType.DMA((8,)),
             pltpu.SemaphoreType.DMA((8,)),
@@ -433,8 +517,9 @@
             jax.ShapeDtypeStruct((1, ATOMS), F32),
             jax.ShapeDtypeStruct((3, 1, ATOMS), F32),
         ),
-        in_specs=[vmem],
-        out_specs=(vmem, vmem),
+        in_specs=[hbm],
+        out_specs=(hbm, hbm),
+        scratch_shapes=[pltpu.SemaphoreType.DMA((2,))],
     )(both)
     return energy[None], forces.reshape(1, 1, 3, ATOMS)
 

time: 48.6 us -> 44.5 us (0.916)
  Pallas kernels: 47.8 us -> 43.6 us
    pallas_call x1, Pallas kernels: 46.6 us -> 42.3 us  [shards(): pl.pallas_call(kernel, out_shape=jax.ShapeDtypeStruct((4, 1, ATOMS), F32)...]
where the time goes in v3:
time: 44.5 us; the launch traced here: 44.4 us
  Pallas kernels  43.6 us (98%)
  between operations  0.82 us (2%)
    pallas_call x1, Pallas kernels, shards(): pl.pallas_call(kernel, out_shape=jax.ShapeDtypeStruct((4, 1, ATOMS), F32)...  42.3 us
    pallas_call x1, Pallas kernels, shards(): pl.pallas_call(hand_over, out_shape=(jax.ShapeDtypeStruct((1, ATOMS), F32...  1.24 us

profile of v3, /device:TPU:1, one launch (start us, length us, event | category | flops | bytes accessed | tf_op | source)
XLA Modules:
  0.0 44.4 jit_solution(7106316473668743168)
XLA Ops:
  0.6 42.3 %shard_map.158.both = f32[4,1,256]{2,1,0:T(1,128)} custom-call(bf16[256,256]{1,0:T(8,128)(2,1)} %bitcast.15, f32[3,1,2048]{2,1,0:T(1,128)} %bitcast.17, s32[1,2048]{1,0:T(1,128)} %bitcast.18, s32[1,256]{1,0:T(1,128)} %bitcast.21, s32[1,256]{1,0:T(1,128)} %bitcast.22, s32[8,192]{1,0:T(8,128)} %bitcast.19, s32[1,8]{1,0:T(1,128)} %bitcast.24, ...), custom_call_target="tpu_custom_call" | custom-call | flops 14000000000 | bytes 4000000 | tf_op jit(solution)/shard_map/pallas_call | solution.py:443
  43.0 1.2 %shard_map.159 = (f32[1,256]{1,0:T(1,128)}, f32[3,1,256]{2,1,0:T(1,128)}) custom-call(f32[4,1,256]{2,1,0:T(1,128)} %shard_map.158.both), custom_call_target="tpu_custom_call" | custom-call | tf_op jit(solution)/shard_map/pallas_call | solution.py:514

commit v4 on v3

--- a/solution.py
+++ b/solution.py
@@ -109,17 +109,28 @@
     core = lax.rem(qy, 2)
     side = 2 * core - 1
     order = [
+        (4 - core, peer(0, -side), 0),
+        (6 + side, peer(1, side), 1),
+        (1 + side, peer(-1, side), 2),
+        (3 + core, peer(0, side), 3),
+        (6 - side, peer(1, -side), 4),
+        (1 - side, peer(-1, -side), 5),
+        (6, peer(1, 0), 6),
+        (1, peer(-1, 0), 7),
+    ]
+    origin = [
+        (4 - core, peer(0, -side)),
+        (1 + side, peer(-1, side)),
         (6 + side, peer(1, side)),
-        (1 + side, peer(-1, side)),
         (3 + core, peer(0, side)),
+        (1 - side, peer(-1, -side)),
         (6 - side, peer(1, -side)),
-        (1 - side, peer(-1, -side)),
+        (1, peer(-1, 0)),
         (6, peer(1, 0)),
-        (1, peer(-1, 0)),
-        (4 - core, peer(0, -side)),
     ]
+    base = [(ATOMS + GHOSTS * block + jnp.int32(0)).astype(F32) for block, _ in origin]
     barrier = pltpu.get_barrier_semaphore()
-    for _, device in order:
+    for _, device, _ in order:
         pl.semaphore_signal(barrier, inc=1, device_id=device, device_id_type=MESH)
 
     pairs = (
@@ -160,13 +171,13 @@
         outg[num] = dot(hit[0:GHOSTS], feat[...]).astype(BF16)
     pl.semaphore_wait(barrier, 8)
     sends = []
-    for num, peer in order:
+    for num, device, place in order:
         copy = pltpu.make_async_remote_copy(
             src_ref=outg.at[num],
-            dst_ref=ghost.at[7 - num],
-            send_sem=send_sem.at[num],
-            recv_sem=recv_sem.at[7 - num],
-            device_id=peer,
+            dst_ref=ghost.at[place],
+            send_sem=send_sem.at[place],
+            recv_sem=recv_sem.at[place],
+            device_id=device,
             device_id_type=MESH,
         )
         copy.start()
@@ -242,18 +253,20 @@
     def before(k, carry):
         lanes = pl.ds(pl.multiple_of(k * 256, 256), 256)
         ids = dsp[3, pl.ds(k, 1), :]
-        for part in range(7):
-            oh[part * 256 : (part + 1) * 256, lanes] = one_hot(row_id + (part * 256.0) == ids)
+        oh[0:ATOMS, lanes] = one_hot(row_id == ids)
+        inside = ids
+        place = jnp.full((1, ATOMS), 16.0, F32)
+        for num in range(8):
+            start = ATOMS + num * GHOSTS
+            away = ids - base[num]
+            oh[start : start + GHOSTS, lanes] = one_hot(row_id[0:GHOSTS] == away)
+            hit = (away >= 0.0) & (away < float(GHOSTS))
+            inside = jnp.where(hit, away, inside)
+            place = jnp.where(hit, 2.0 * num, place)
         rows[:, lanes] = dot(feat_t, oh[0:256, lanes]).astype(BF16)
-        own = ids < float(ATOMS)
-        block = jnp.zeros((1, ATOMS), F32)
-        for num in range(1, 8):
-            block = block + jnp.where(ids >= float(ATOMS + num * GHOSTS), 1.0, 0.0)
-        inside = jnp.where(own, ids, ids - float(ATOMS) - block * float(GHOSTS))
         upper = jnp.where(inside >= 128.0, 1.0, 0.0)
         low_hot[:, lanes] = one_hot(row_id[0:128] == inside - 128.0 * upper)
-        part_id = jnp.where(own, 16.0, 2.0 * block) + upper
-        high_hot[:, lanes] = one_hot(row_id[0:32] == part_id)
+        high_hot[:, lanes] = one_hot(row_id[0:32] == place + upper)
         offset = (geo[4, pl.ds(k, 1), :] - centre_at) * 4.0
         basis = jnp.where(unit_id < 8, jnp.exp(-offset * offset), 0.0)
         both = jnp.concatenate([basis, -8.0 * offset * basis], axis=1).astype(BF16)
@@ -267,22 +280,25 @@
 
     lax.fori_loop(0, SLOTS, before, 0)
 
-    def take(num):
-        turned = jnp.transpose(ghost[num])
-        first = pl.multiple_of(ATOMS + num * GHOSTS, 64)
+    def landed_rows(start, stop):
+        for num in range(start, stop):
+            sends[num].wait_recv()
+        return jnp.transpose(
+            jnp.concatenate([ghost[num] for num in range(start, stop)], axis=0)
+        )
+
+    for start, stop in ((0, 1), (1, 4), (4, 8)):
+        turned = landed_rows(start, stop)
+        ids = slice(ATOMS + start * GHOSTS, ATOMS + stop * GHOSTS)
         for part in range(4):
             here = slice(part * 512, (part + 1) * 512)
-            found = dot(turned, oh[pl.ds(first, GHOSTS), here])
-            rows[:, here] = rows[:, here] + found.astype(BF16)
-
+            rows[:, here] = rows[:, here] + dot(turned, oh[ids, here]).astype(BF16)
     for copy in sends:
         copy.wait_send()
-    for copy in (2, 5, 6, 1, 0, 7, 4, 3):
-        sends[copy].wait_recv()
-        take(7 - order[copy][0])
 
     def first(k, at):
-        found = rows[:, k * 256 : (k + 1) * 256]
+        lanes = slice(k * 256, (k + 1) * 256)
+        found = rows[:, lanes]
         for part in range(4):
             here = slice(part * 256, (part + 1) * 256)
             act, slope = silu_pair(dot(wnt[here, :], found) + pre[k, here, :])
@@ -298,7 +314,6 @@
             act2[here, at + 256 : at + 512] = (slope * hidden[:, 256:]).astype(BF16)
 
     def product(k, weight, sums):
-        tws[k] = weight
         unit = [geo[axis, k : k + 1, :] for axis in range(3)]
         row = rows[:, k * 256 : (k + 1) * 256].astype(F32)
         s, v = row[0:CH], [row[CH * (m + 1) : CH * (m + 2)] for m in range(3)]
@@ -314,9 +329,9 @@
         first(k + 1, 512)
         second(0)
         second(512)
-        weight = dot(wtt[...], act2[...])
-        sums = product(k, weight[:, 0:512], sums)
-        sums = product(k + 1, weight[:, 512:], sums)
+        tws[k // 2] = dot(wtt[...], act2[...])
+    for k in range(SLOTS):
+        sums = product(k, tws[k // 2, :, (k % 2) * 512 : (k % 2) * 512 + 512], sums)
 
     eye = iota((CH, CH), 0) == iota((CH, CH), 1)
     read = jnp.sum(jnp.where(eye, ro[...], 0.0), axis=1, keepdims=True)
@@ -331,7 +346,7 @@
         env = geo[3, pl.ds(k, 1), :]
         row = rows[:, lanes].astype(F32)
         s, v = row[0:CH], [row[CH * (m + 1) : CH * (m + 2)] for m in range(3)]
-        weight = tws[k]
+        weight = tws[k // 2, :, (k % 2) * 512 : (k % 2) * 512 + 512]
         tw, dtw = weight[:, :256], weight[:, 256:]
         q = cot[0] * (s + unit[0] * v[0] + unit[1] * v[1] + unit[2] * v[2])
         for m in range(3):
@@ -377,12 +392,13 @@
             axis=0,
         )
     returns = []
-    for num, device in order:
+    for place in (1, 2, 3, 4, 5, 6, 7, 0):
+        block, device = origin[place]
         copy = pltpu.make_async_remote_copy(
-            src_ref=back_out.at[num],
-            dst_ref=back_in.at[7 - num],
-            send_sem=bsend_sem.at[num],
-            recv_sem=brecv_sem.at[7 - num],
+            src_ref=back_out.at[place],
+            dst_ref=back_in.at[7 - block],
+            send_sem=bsend_sem.at[place],
+            recv_sem=brecv_sem.at[7 - block],
             device_id=device,
             device_id_type=MESH,
         )
@@ -479,7 +495,7 @@
             pltpu.VMEM((WIDTH, EDGES), BF16),
             pltpu.VMEM((HID, 4 * ATOMS), BF16),
             pltpu.VMEM((HID, 4 * ATOMS), BF16),
-            pltpu.VMEM((SLOTS, CH, 2 * ATOMS), F32),
+            pltpu.VMEM((SLOTS // 2, CH, 4 * ATOMS), F32),
             pltpu.VMEM((8, 8, 128), F32),
             pltpu.VMEM((8, 8, 128), F32),
             pltpu.SemaphoreType.DMA((15,)),

time: 44.5 us -> 42.4 us (0.953)
  Pallas kernels: 43.6 us -> 41.4 us
    pallas_call x1, Pallas kernels: 42.3 us -> 40.2 us  [shards(): pl.pallas_call(kernel, out_shape=jax.ShapeDtypeStruct((4, 1, ATOMS), F32)...]
where the time goes in v4:
time: 42.4 us; the launch traced here: 42.2 us
  Pallas kernels  41.4 us (98%)
  between operations  0.8 us (2%)
    pallas_call x1, Pallas kernels, shards(): pl.pallas_call(kernel, out_shape=jax.ShapeDtypeStruct((4, 1, ATOMS), F32)...  40.2 us
    pallas_call x1, Pallas kernels, shards(): pl.pallas_call(hand_over, out_shape=(jax.ShapeDtypeStruct((1, ATOMS), F32...  1.24 us

profile of v4, /device:TPU:1, one launch (start us, length us, event | category | flops | bytes accessed | tf_op | source)
XLA Modules:
  0.0 42.2 jit_solution(4409874749788974373)
XLA Ops:
  0.6 40.2 %shard_map.158.both = f32[4,1,256]{2,1,0:T(1,128)} custom-call(bf16[256,256]{1,0:T(8,128)(2,1)} %bitcast.15, f32[3,1,2048]{2,1,0:T(1,128)} %bitcast.17, s32[1,2048]{1,0:T(1,128)} %bitcast.18, s32[1,256]{1,0:T(1,128)} %bitcast.21, s32[1,256]{1,0:T(1,128)} %bitcast.22, s32[8,192]{1,0:T(8,128)} %bitcast.19, s32[1,8]{1,0:T(1,128)} %bitcast.24, ...), custom_call_target="tpu_custom_call" | custom-call | flops 14000000000 | bytes 4000000 | tf_op jit(solution)/shard_map/pallas_call | solution.py:459
  40.8 1.2 %shard_map.159 = (f32[1,256]{1,0:T(1,128)}, f32[3,1,256]{2,1,0:T(1,128)}) custom-call(f32[4,1,256]{2,1,0:T(1,128)} %shard_map.158.both), custom_call_target="tpu_custom_call" | custom-call | tf_op jit(solution)/shard_map/pallas_call | solution.py:530

commit v5 on v4

--- a/solution.py
+++ b/solution.py
@@ -130,7 +130,7 @@
     ]
     base = [(ATOMS + GHOSTS * block + jnp.int32(0)).astype(F32) for block, _ in origin]
     barrier = pltpu.get_barrier_semaphore()
-    for _, device, _ in order:
+    for _, device, _ in order[1:] + order[:1]:
         pl.semaphore_signal(barrier, inc=1, device_id=device, device_id_type=MESH)
 
     pairs = (
@@ -293,15 +293,14 @@
         for part in range(4):
             here = slice(part * 512, (part + 1) * 512)
             rows[:, here] = rows[:, here] + dot(turned, oh[ids, here]).astype(BF16)
-    for copy in sends:
-        copy.wait_send()
 
     def first(k, at):
         lanes = slice(k * 256, (k + 1) * 256)
         found = rows[:, lanes]
+        summed = dot(wnt[...], found)
         for part in range(4):
             here = slice(part * 256, (part + 1) * 256)
-            act, slope = silu_pair(dot(wnt[here, :], found) + pre[k, here, :])
+            act, slope = silu_pair(summed[here] + pre[k, here, :])
             act1[here, at : at + 256] = act.astype(BF16)
             act1[here, at + 256 : at + 512] = (slope * drad[k, here, :]).astype(BF16)
 
@@ -421,7 +420,7 @@
     both = dot(jnp.concatenate(split(back), axis=0), sel[...])
     both = both[0:8] + both[8:16]
     total = total + both[0:3, 0:ATOMS] + both[4:7, ATOMS:]
-    for copy in returns:
+    for copy in sends + returns:
         copy.wait_send()
     for axis in range(3):
         out_ref[axis] = total[axis : axis + 1]

time: 42.4 us -> 42.5 us (level)
  no operation moved by 1% of the time
where the time goes in v5:
time: 42.5 us; the launch traced here: 42.4 us
  Pallas kernels  41.6 us (98%)
  between operations  0.8 us (2%)
    pallas_call x1, Pallas kernels, shards(): pl.pallas_call(kernel, out_shape=jax.ShapeDtypeStruct((4, 1, ATOMS), F32)...  40.3 us
    pallas_call x1, Pallas kernels, shards(): pl.pallas_call(hand_over, out_shape=(jax.ShapeDtypeStruct((1, ATOMS), F32...  1.24 us

profile of v5, /device:TPU:1, one launch (start us, length us, event | category | flops | bytes accessed | tf_op | source)
XLA Modules:
  0.0 42.4 jit_solution(17610998853968409341)
XLA Ops:
  0.6 40.3 %shard_map.158.both = f32[4,1,256]{2,1,0:T(1,128)} custom-call(bf16[256,256]{1,0:T(8,128)(2,1)} %bitcast.15, f32[3,1,2048]{2,1,0:T(1,128)} %bitcast.17, s32[1,2048]{1,0:T(1,128)} %bitcast.18, s32[1,256]{1,0:T(1,128)} %bitcast.21, s32[1,256]{1,0:T(1,128)} %bitcast.22, s32[8,192]{1,0:T(8,128)} %bitcast.19, s32[1,8]{1,0:T(1,128)} %bitcast.24, ...), custom_call_target="tpu_custom_call" | custom-call | flops 14000000000 | bytes 4000000 | tf_op jit(solution)/shard_map/pallas_call | solution.py:458
  41.0 1.2 %shard_map.159 = (f32[1,256]{1,0:T(1,128)}, f32[3,1,256]{2,1,0:T(1,128)}) custom-call(f32[4,1,256]{2,1,0:T(1,128)} %shard_map.158.both), custom_call_target="tpu_custom_call" | custom-call | tf_op jit(solution)/shard_map/pallas_call | solution.py:529
